TPU v7x, 128 devices: a whole 4x4x4 slice. The times are simulated.
128 devices in a mesh: dp: 8 (over z_hi, y), ctx: 16 (over x, z_lo, core).
Axes of the slice: x: 4, y: 4, z: 4 (z_hi: 2, z_lo: 2; z = z_hi * 2 + z_lo), core: 2. Of those that a mesh axis runs over, the one named last changes fastest.
Arguments:
- queries: bfloat16 [8, 2048, 4096], P('dp', 'ctx'), may hold values from -6 to 6
- keys: bfloat16 [8, 2048, 512], P('dp', 'ctx'), may hold values from -6 to 6
- values: bfloat16 [8, 2048, 512], P('dp', 'ctx'), may hold values from -6 to 6
- saved: bfloat16 [8, 2048, 4096], P('dp', 'ctx'), may hold values from -6 to 6
- out_grad: bfloat16 [8, 2048, 4096], P('dp', 'ctx'), may hold values from -6 to 6
- doc_ids: int32 [8, 2048], P('dp', 'ctx'), may hold values from 0 to 2, never falling along the last dimension, each value on 1 to 1024 neighbouring positions
- inputs: bfloat16 [8, 2048, 4096], P('dp', 'ctx'), may hold values from -6 to 6
- bmat: bfloat16 [8, 2048, 512], P('dp', 'ctx'), may hold values from -1.1953125 to 1.1953125
- cmat: bfloat16 [8, 2048, 512], P('dp', 'ctx'), may hold values from -1.1953125 to 1.1953125
- step: float32 [8, 2048, 128], P('dp', 'ctx'), may hold values from 0.25 to 1
- alog: float32 [128], replicated, may hold values from -9 to -3
- skip: float32 [128], replicated, may hold values from 0.5 to 1.5
Outputs:
- grad_keys: bfloat16 [8, 2048, 512], P('dp', 'ctx')
- grad_values: bfloat16 [8, 2048, 512], P('dp', 'ctx')
- grad_inputs: bfloat16 [8, 2048, 4096], P('dp', 'ctx')
- grad_decay: float32 [2, 128], replicated
Inputs may be any that keep to these rules, and one draw needn't show every extreme that they name: `doc_ids`: numbers never fall along a sequence; each document has at least one position and one has exactly 1024.
All inputs are finite; a program needn't handle non-finite values.
Results may differ from a plain program's by a relative error of at most 0.0045.
The roundings to bfloat16 on the way count: a program that leaves them out, or rounds other values in their place, can miss the bound.
Values may be sent and summed in bfloat16 or wider, within the bound.
A program may use at most 256 MiB of HBM per device.

v0:
```python
import jax
import jax.numpy as jnp
from jax import lax
from jax.sharding import PartitionSpec as P

QHEADS = 32
KVHEADS = 4
HEAD_DIM = 128
SSM_HEADS = 128
SSM_DIM = 32
STATE = 128


HIGHEST = lax.Precision.HIGHEST


def partner(array, axis, bit):
    return lax.ppermute(array, axis, [(i, i ^ 1 << bit) for i in range(lax.axis_size(axis))])


def carried_in(array, axis, join, neutral):
    place = lax.axis_index(axis)
    gathered = jax.tree.map(
        lambda a, kind: lax.all_gather(a.astype(kind), axis), array, (jnp.bfloat16, jnp.bfloat16)
    )
    state = jax.tree.map(lambda a, e: jnp.zeros_like(a) + jnp.asarray(e, a.dtype), array, neutral)

    def one(step, state):
        return join(
            state,
            jax.tree.map(
                lambda a, own: lax.dynamic_index_in_dim(a, step, 0, False).astype(own.dtype),
                gathered,
                array,
            ),
        )

    return lax.fori_loop(0, place, one, state)


def entering_2(array, axis, combine, identity):
    length, index = (lax.axis_size(axis), lax.axis_index(axis))
    everything = jax.tree.map(lambda part: lax.all_gather(part, axis), array)
    start = jax.tree.map(
        lambda part, zero: jnp.broadcast_to(jnp.asarray(zero, part.dtype), part.shape),
        array,
        identity,
    )

    def step(k, before):
        at = length - 1 - k
        reached = at > index
        new = combine(before, jax.tree.map(lambda part: part[at], everything))
        return jax.tree.map(lambda a, b: jnp.where(reached, a, b), new, before)

    return lax.fori_loop(0, length, step, start)


def storage_positions(rows, per_dev, count):
    half = per_dev // 2
    device = rows // per_dev
    within = rows % per_dev
    block = jnp.where(within < half, device, 2 * count - 1 - device)
    return block * half + within % half


def span_whole(step, keep, alog):
    total = jnp.cumsum(-step * jnp.exp(alog)[None, :], axis=0)
    resets = jnp.cumsum(1.0 - keep)
    return jnp.exp(total[-1]) * (resets[-1] == 0).astype(jnp.float32)


def ssd_span(inputs, bmat, cmat, step, keep, alog, skip, h_in):
    rows = inputs.shape[0]
    heads = alog.shape[0]
    groups = bmat.shape[1] // STATE
    ratio = heads // groups
    total = jnp.cumsum(-step * jnp.exp(alog)[None, :], axis=0)
    resets = jnp.cumsum(1.0 - keep)
    xheads = inputs.reshape(rows, heads, -1)
    b_narrow = bmat.reshape(rows, groups, STATE)
    c_narrow = cmat.reshape(rows, groups, STATE)
    bgroup = b_narrow.astype(jnp.float32)
    cgroup = c_narrow.astype(jnp.float32)
    bheads = jnp.repeat(bgroup, ratio, axis=1)
    cheads = jnp.repeat(cgroup, ratio, axis=1)
    order = jnp.arange(rows)
    same = (order[:, None] >= order[None, :]) & (resets[:, None] == resets[None, :])
    diff = total[:, None, :] - total[None, :, :]
    lmat = jnp.where(same[:, :, None], jnp.exp(jnp.where(same[:, :, None], diff, 0.0)), 0.0)
    inner = jnp.einsum("tgn,sgn->tsg", c_narrow, b_narrow, preferred_element_type=jnp.float32)
    inner = jnp.repeat(inner, ratio, axis=2)
    weights = inner * lmat * step[None, :, :]
    intra = jnp.einsum("tsh,shp->thp", weights, xheads, precision=HIGHEST)
    entry = jnp.exp(total) * (resets == 0).astype(jnp.float32)[:, None]
    carried = jnp.einsum("hpn,thn->thp", h_in, cheads, precision=HIGHEST) * entry[:, :, None]
    output = intra + carried + skip[None, :, None] * xheads
    tail = jnp.exp(total[-1][None, :] - total) * (resets == resets[-1]).astype(jnp.float32)[:, None]
    whole = jnp.exp(total[-1]) * (resets[-1] == 0).astype(jnp.float32)
    fresh = jnp.einsum(
        "shp,shn->hpn", (tail * step)[:, :, None] * xheads, bheads, precision=HIGHEST
    )
    h_out = whole[:, None, None] * h_in + fresh
    return (output.reshape(rows, -1), h_out)


def group_terms(qgroup, dgroup, ogroup, kgroup, vgroup, mask):
    scale = HEAD_DIM ** (-0.5)
    scores = jnp.einsum("qhd,kd->hqk", qgroup, kgroup, preferred_element_type=jnp.float32) * scale
    lse = jax.nn.logsumexp(jnp.where(mask[None], scores, -jnp.inf), axis=-1)
    delta = jnp.sum(dgroup.astype(jnp.float32) * ogroup.astype(jnp.float32), axis=-1).T
    probs = jnp.where(mask[None], jnp.exp(scores - lse[:, :, None]), 0.0)
    dprobs = jnp.einsum("qhd,kd->hqk", dgroup, vgroup, preferred_element_type=jnp.float32)
    dscores = (probs * (dprobs - delta[:, :, None]) * scale).astype(jnp.bfloat16)
    return (probs.astype(jnp.bfloat16), dscores)


def forward_combine(earlier, later):
    return (earlier[0] * later[0], later[0][:, None, None] * earlier[1] + later[1])


def backward_combine(earlier, later):
    return (earlier[0] * later[0], later[1] + later[0][:, None, None] * earlier[1])


def shards(queries, keys, values, saved, out_grad, doc_ids, inputs, bmat, cmat, step, alog, skip):
    count = lax.axis_size("ctx")
    device = lax.axis_index("ctx")
    rows = queries.shape[1]
    half = rows // 2
    ratio = QHEADS // KVHEADS
    width = ratio * HEAD_DIM
    ids_local = doc_ids[0]
    keys_all, values_all, ids_all = (
        lax.all_gather(keys[0], "ctx", axis=0, tiled=True),
        lax.all_gather(values[0], "ctx", axis=0, tiled=True),
        lax.all_gather(ids_local, "ctx", axis=0, tiled=True),
    )
    seq_len = rows * count
    own_pos = storage_positions(device * rows + jnp.arange(rows, dtype=jnp.int32), rows, count)
    key_pos = storage_positions(jnp.arange(seq_len, dtype=jnp.int32), rows, count)
    own_docs = jnp.take(ids_all, own_pos)
    key_docs = jnp.take(ids_all, key_pos)
    mask = (key_pos[None, :] <= own_pos[:, None]) & (key_docs[None, :] == own_docs[:, None])
    q_rows = queries[0]
    d_rows = out_grad[0]
    o_rows = saved[0]
    grad_q_parts = []
    tiles = []
    for group in range(KVHEADS):
        qgroup = q_rows[:, group * width : (group + 1) * width].reshape(rows, ratio, HEAD_DIM)
        dgroup = d_rows[:, group * width : (group + 1) * width].reshape(rows, ratio, HEAD_DIM)
        ogroup = o_rows[:, group * width : (group + 1) * width].reshape(rows, ratio, HEAD_DIM)
        kgroup = keys_all[:, group * HEAD_DIM : (group + 1) * HEAD_DIM]
        vgroup = values_all[:, group * HEAD_DIM : (group + 1) * HEAD_DIM]
        probs_b, dscores = group_terms(qgroup, dgroup, ogroup, kgroup, vgroup, mask)
        grad_q_parts.append(
            jnp.einsum("hqk,kd->qhd", dscores, kgroup, preferred_element_type=jnp.float32).reshape(
                rows, width
            )
        )
        tiles.append((qgroup, dgroup, probs_b, dscores))
    key_terms = []
    value_terms = []
    for qgroup, dgroup, probs_b, dscores in tiles:
        key_terms.append(
            jnp.einsum("hqk,qhd->kd", dscores, qgroup, preferred_element_type=jnp.float32)
        )
        value_terms.append(
            jnp.einsum("hqk,qhd->kd", probs_b, dgroup, preferred_element_type=jnp.float32)
        )
    term = jnp.concatenate(key_terms + value_terms, axis=1)
    summed = lax.psum_scatter(term, "ctx", scatter_dimension=0, tiled=True)
    kv_width = KVHEADS * HEAD_DIM
    grad_keys = summed[:, :kv_width].astype(jnp.bfloat16)[None]
    grad_values = summed[:, kv_width:].astype(jnp.bfloat16)[None]
    grad_q = jnp.concatenate(grad_q_parts, axis=1).astype(jnp.bfloat16)
    first_half = grad_q[:half]
    second_half = grad_q[half:]
    levels = count.bit_length() - 1
    for level in range(levels):
        second_half = partner(second_half, "ctx", level)
    for level in reversed(range(levels)):
        low_bit = device // (1 << level) % 2
        leaving_half = jnp.where(low_bit == 0, second_half, first_half)
        arrived = partner(leaving_half, "ctx", level)
        first_half = jnp.where(low_bit == 1, arrived, first_half)
        second_half = jnp.where(low_bit == 0, arrived, second_half)
    cotangent = jnp.concatenate([first_half, second_half], axis=0)
    before = lax.dynamic_index_in_dim(ids_all, jnp.maximum(device * rows - 1, 0), 0, keepdims=False)
    before = jnp.where(device > 0, before, -1)
    previous = jnp.concatenate([before[None].astype(jnp.int32), ids_local[:-1]])
    keep = (ids_local == previous).astype(jnp.float32)
    inputs32 = inputs[0].astype(jnp.float32)
    b_rows = bmat[0]
    c_rows = cmat[0]
    s_rows = step[0]
    empty_state = jnp.zeros((SSM_HEADS, SSM_DIM, STATE), jnp.float32)
    _, local_state = ssd_span(inputs32, b_rows, c_rows, s_rows, keep, alog, skip, empty_state)
    whole = span_whole(s_rows, keep, alog)
    unity = jnp.ones((SSM_HEADS,), jnp.float32)
    _, entering = carried_in((whole, local_state), "ctx", forward_combine, (unity, empty_state))

    def local_layer(inputs_in, alog_in, skip_in, state_in):
        return ssd_span(inputs_in, b_rows, c_rows, s_rows, keep, alog_in, skip_in, state_in)

    _, pullback = jax.vjp(local_layer, inputs32, alog, skip, entering)
    upstream = cotangent.astype(jnp.float32)
    grad_x1, grad_a1, grad_s1, grad_entry = pullback((upstream, empty_state))
    _, leaving = entering_2((whole, grad_entry), "ctx", backward_combine, (unity, empty_state))
    grad_x2, grad_a2, grad_s2, _ = pullback((jnp.zeros_like(upstream), leaving))
    grad_inputs = (grad_x1 + grad_x2).astype(jnp.bfloat16)[None]
    grad_decay = lax.psum(jnp.stack([grad_a1 + grad_a2, grad_s1 + grad_s2]), ("dp", "ctx"))
    return (grad_keys, grad_values, grad_inputs, grad_decay)


def solution(mesh):
    return jax.shard_map(
        shards,
        mesh=mesh,
        in_specs=(
            P("dp", "ctx", None),
            P("dp", "ctx", None),
            P("dp", "ctx", None),
            P("dp", "ctx", None),
            P("dp", "ctx", None),
            P("dp", "ctx"),
            P("dp", "ctx", None),
            P("dp", "ctx", None),
            P("dp", "ctx", None),
            P("dp", "ctx", None),
            P(),
            P(),
        ),
        out_specs=(P("dp", "ctx", None), P("dp", "ctx", None), P("dp", "ctx", None), P()),
        check_vma=False,
    )
```

profile of v0, /device:TPU:1, one launch (start us, length us, event | category | flops | bytes accessed | tf_op | source)
XLA Modules:
  0.0 731.0 jit_solution(14696529384194228024)
XLA Ops:
  16.5 21.4 %all-gather = s32[1,2048]{1,0:T(1,128)S(1)} all-gather(s32[1,128]{1,0:T(1,128)S(1)} %copy-done.64), channel_id=2, replica_groups=mesh['dp'=8,'ctx'=16] {'ctx'}, dimensions={1}, use_global_device_ids=true | all-gather | bytes 8704 | tf_op jit(solution)/shard_map/all_gather | solution.py:137
  39.1 11.8 %gather_fusion = s32[2048]{0:T(1024)S(1)} fusion(s32[2048]{0:T(1024)S(1)} %bitcast.400, s32[2048]{0:T(1024)S(1)} %broadcast_clamp_fusion), kind=kCustom, calls=%fused_computation | custom fusion | bytes 24576 | tf_op jit(solution)/shard_map/jit(_take)/gather | solution.py:143
  61.3 12.6 %exponential_reduce_fusion = (f32[8,128]{1,0:T(8,128)S(1)}, f32[8,128]{1,0:T(8,128)S(1)}, f32[8,128]{1,0:T(8,128)S(1)}, f32[8,128]{1,0:T(8,128)S(1)}, f32[2048,128,8]{1,0,2:T(8,128)}) fusion(f32[2048,128,8]{1,0,2:T(8,128)} %get-tuple-element.293, f32[8,128]{1,0:T(8,128)S(1)} %is-finite_select_fusion, pred[128,2048]{0,1:T(8,128)(4,1)S(1)} %compare_and_fusion, ...), kind=kOutput, calls=%fused_computation.50 | convolution fusion | flops 566226944 | bytes 34627584 | tf_op jit(solution)/shard_map/qhd,kd->hqk/dot_general | solution.py:109
  73.9 5.7 exponential_reduce_fusion.1
  83.1 5.5 fusion.8
  91.5 6.5 fusion.13
  102.6 6.5 fusion.18
  114.4 6.5 fusion.23
  124.3 10.3 %copy.141 = bf16[128,1024]{1,0:T(8,128)(2,1)S(1)} copy(bf16[128,1024]{0,1:T(8,128)(2,1)} %bitcast.452) | data formatting | bytes 524288 | tf_op jit(solution)/shard_map/reshape | solution.py:158
  138.4 12.5 %collective-permute-done.1 = bf16[64,4096]{1,0:T(8,128)(2,1)S(1)} collective-permute-done((bf16[64,4096]{1,0:T(8,128)(2,1)S(1)}, bf16[64,4096]{1,0:T(8,128)(2,1)S(1)}, u32[]{:S(2)}, u32[]{:S(2)}) %collective-permute-start.1) | collective-permute-done | bytes 524320 | tf_op jit(solution)/shard_map/ppermute | solution.py:18
  151.7 11.5 %collective-permute-done.2 = bf16[64,4096]{1,0:T(8,128)(2,1)S(1)} collective-permute-done((bf16[64,4096]{1,0:T(8,128)(2,1)S(1)}, bf16[64,4096]{1,0:T(8,128)(2,1)S(1)}, u32[]{:S(2)}, u32[]{:S(2)}) %collective-permute-start.2) | collective-permute-done | bytes 524320 | tf_op jit(solution)/shard_map/ppermute | solution.py:18
  165.0 11.1 %collective-permute-done.3 = bf16[64,4096]{1,0:T(8,128)(2,1)S(1)} collective-permute-done((bf16[64,4096]{1,0:T(8,128)(2,1)S(1)}, bf16[64,4096]{1,0:T(8,128)(2,1)S(1)}, u32[]{:S(2)}, u32[]{:S(2)}) %collective-permute-start.3) | collective-permute-done | bytes 524320 | tf_op jit(solution)/shard_map/ppermute | solution.py:18
  178.1 10.2 %collective-permute-done.4 = bf16[64,4096]{1,0:T(8,128)(2,1)S(1)} collective-permute-done((bf16[64,4096]{1,0:T(8,128)(2,1)S(1)}, bf16[64,4096]{1,0:T(8,128)(2,1)S(1)}, u32[]{:S(2)}, u32[]{:S(2)}) %collective-permute-start.4) | collective-permute-done | bytes 524320 | tf_op jit(solution)/shard_map/ppermute | solution.py:18
  190.0 9.0 %collective-permute-done.5 = bf16[64,4096]{1,0:T(8,128)(2,1)S(1)} collective-permute-done((bf16[64,4096]{1,0:T(8,128)(2,1)}, bf16[64,4096]{1,0:T(8,128)(2,1)S(1)}, u32[]{:S(2)}, u32[]{:S(2)}) %collective-permute-start.5) | collective-permute-done | bytes 524320 | tf_op jit(solution)/shard_map/ppermute | solution.py:18
  203.1 5.9 collective-permute-done.6
  209.1 5.8 collective-permute-start.7
  227.7 9.0 %fusion.89 = f32[128,32,128]{2,1,0:T(8,128)} fusion(f32[128,128,128]{2,0,1:T(8,128)S(1)} %bitcast.404, f32[128,128]{0,1:T(8,128)S(1)} %copy-done.48, f32[128]{0:T(128)S(1)} %copy-done.66, bf16[64,128,32]{0,2,1:T(8,128)(2,1)S(1)} %bitcast.414, bf16[64,128,32]{0,2,1:T(8,128)(2,1)S(1)} %bitcast.417), kind=kOutput, calls=%fused_computation.119 | convolution fusion | flops 808452096 | bytes 11600384 | tf_op jit(solution)/shard_map/transpose(jvp(hpn,thn->thp))/dot_general | solution.py:96
  265.0 17.1 %all-gather.5 = f32[16,1,128]{2,1,0:T(1,128)S(1)} all-gather(f32[1,1,128]{2,1,0:T(1,128)S(1)} %get-tuple-element.289), channel_id=1, replica_groups=mesh['dp'=8,'ctx'=16] {'ctx'}, dimensions={0}, use_global_device_ids=true | all-gather | bytes 8704 | tf_op jit(solution)/shard_map/all_gather | solution.py:43
  286.3 14.5 %fusion.95 = f32[128,32,128]{2,1,0:T(8,128)} fusion(f32[128,128,128]{2,0,1:T(8,128)S(1)} %bitcast.401), kind=kOutput, calls=%fused_computation.131 | convolution fusion | flops 805306368 | bytes 10485760 | tf_op jit(solution)/shard_map/transpose(jvp(shp,shn->hpn))/dot_general | solution.py:100
  300.8 105.7 %all-gather.16.cloned.1.call-done = f32[2048,32,128]{2,1,0:T(8,128)} async-done(((f32[128,32,128]{2,1,0:T(8,128)}), f32[2048,32,128]{2,1,0:T(8,128)}) %all-gather.16.cloned.1.call-update) | async-done | bytes 33554448 | tf_op jit(solution)/shard_map/all_gather | solution.py:43
  406.4 36.1 %while.29 = (s32[]{:T(128)}, f32[128,32,128]{2,1,0:T(8,128)S(1)}, s32[]{:T(128)}, f32[16,128,32,128]{3,2,1,0:T(8,128)}, f32[16,128]{1,0:T(8,128)S(1)}, /*index=5*/s32[]{:T(128)}, s32[]{:T(128)}, s32[]{:T(128)}, s32[]{:T(128)}) while((s32[]{:T(128)}, f32[128,32,128]{2,1,0:T(8,128)S(1)}, s32[]{:T(128)}, ...), condition=%wide.region_16.17_spmd.clone, body=%wide.region_15.16_spmd.clone.sunk | while | flops 2097160 | bytes 6293167 | solution.py:56
  442.5 18.1 %fusion.86 = (f32[128,128]{0,1:T(8,128)}, f32[128,128]{0,1:T(8,128)}, f32[128,32,128]{2,1,0:T(8,128)}) fusion(bf16[128,128,32]{0,2,1:T(8,128)(2,1)S(1)} %bitcast.410, f32[128,32,128]{2,1,0:T(8,128)} %fusion.95, f32[128,32,128]{2,1,0:T(8,128)S(1)} %get-tuple-element.180, f32[128,128,128]{2,0,1:T(8,128)} %bitcast.402), kind=kOutput, calls=%fused_computation.109 | convolution fusion | flops 807895040 | bytes 15859712 | tf_op jit(solution)/shard_map/transpose(jvp(shp,shn->hpn))/dot_general | solution.py:100
  466.3 10.5 %add_convert_fusion = bf16[128,32,128]{2,1,0:T(8,128)(2,1)} fusion(f32[128,128,128]{2,0,1:T(8,128)} %bitcast.403, bf16[128,128,32]{0,2,1:T(8,128)(2,1)S(1)} %bitcast.411, f32[128]{0:T(128)S(1)} %copy-done.67, f32[128,128]{0,1:T(8,128)S(1)} %copy.131), kind=kOutput, calls=%fused_computation.118 | convolution fusion | flops 807403520 | bytes 10551808 | tf_op jit(solution)/shard_map/shp,shn->hpn/dot_general | solution.py:100
  478.4 18.8 %all-gather.6 = bf16[16,1,128]{2,1,0:T(2,128)(2,1)S(1)} all-gather(bf16[1,1,128]{2,1,0:T(2,128)(2,1)S(1)} %get-tuple-element.287), channel_id=1, replica_groups=mesh['dp'=8,'ctx'=16] {'ctx'}, dimensions={0}, use_global_device_ids=true | all-gather | bytes 4352 | tf_op jit(solution)/shard_map/all_gather | solution.py:24
  498.6 7.9 %fusion.5 = f32[128,128,128]{1,0,2:T(8,128)} fusion(f32[128,128]{0,1:T(8,128)S(1)} %copy.153, f32[128,128]{0,1:T(8,128)S(1)} %copy.151, f32[128,128,4]{1,0,2:T(8,128)S(1)} %copy.150, pred[128,128]{1,0:T(8,128)(4,1)S(1)} %fusion.108, bf16[128,128,32]{0,2,1:T(8,128)(2,1)S(1)} %bitcast.412), kind=kOutput, calls=%fused_computation.14 | convolution fusion | flops 817889280 | bytes 9846784 | tf_op jit(solution)/shard_map/transpose(jvp(tsh,shp->thp))/dot_general | solution.py:94
  509.7 7.9 %fusion.3 = f32[128,128,128]{1,0,2:T(8,128)} fusion(f32[128,128]{0,1:T(8,128)} %copy-done.37, f32[128,128]{0,1:T(8,128)S(1)} %copy.151, f32[128,128,4]{1,0,2:T(8,128)S(1)} %copy.150, pred[128,128]{1,0:T(8,128)(4,1)S(1)} %fusion.108, bf16[128,32,128]{2,1,0:T(8,128)(2,1)S(1)} %bitcast.422, bf16[128,128,32]{0,2,1:T(8,128)(2,1)S(1)} %bitcast.413), kind=kOutput, calls=%fused_computation.12 | convolution fusion | flops 146800640 | bytes 10895360 | tf_op jit(solution)/shard_map/transpose(jvp(tsh,shp->thp))/dot_general | solution.py:94
  519.6 13.0 %select_reduce_fusion.1 = (f32[128,128]{0,1:T(8,128)}, f32[128,128]{0,1:T(8,128)}, f32[128,128]{0,1:T(8,128)}, f32[128,128]{0,1:T(8,128)}, f32[128,128,128]{1,0,2:T(8,128)}) fusion(f32[128,128,128]{1,0,2:T(8,128)} %fusion.5, pred[128,128]{1,0:T(8,128)(4,1)S(1)} %fusion.108, f32[128,128,128]{1,0,2:T(8,128)} %fusion.3, f32[128,128]{0,1:T(8,128)} %copy-done.37, ...), kind=kLoop, calls=%fused_computation.59 | loop fusion | flops 23003136 | bytes 25837568 | tf_op jit(solution)/shard_map/transpose(jvp())/reduce_sum | solution.py:89
  540.1 9.2 %fusion.145 = f32[128,32,128]{2,1,0:T(8,128)} fusion(bf16[128,32,128]{2,1,0:T(8,128)(2,1)} %bitcast.423, f32[128,128,128]{1,0,2:T(8,128)} %get-tuple-element.290), kind=kOutput, calls=%fused_computation.289 | convolution fusion | flops 805306368 | bytes 11534336 | tf_op jit(solution)/shard_map/transpose(jvp(tsh,shp->thp))/dot_general | solution.py:94
  554.5 10.5 %fusion.79 = bf16[128,128,32]{0,2,1:T(8,128)(2,1)} fusion(f32[128,32,128]{2,1,0:T(8,128)} %get-tuple-element.295, f32[128,32,128]{2,1,0:T(8,128)} %fusion.145, f32[128,32,128]{2,1,0:T(8,128)S(1)} %copy-done.6, f32[128,128,128]{1,0,2:T(8,128)} %get-tuple-element.290, f32[128]{0:T(128)S(1)} %copy-done.70, f32[128]{0:T(128)S(1)} %copy-done.69, ...), kind=kOutput, calls=%fused_computation.103 | convolution fusion | flops 812122112 | bytes 16843776 | tf_op jit(solution)/shard_map/transpose(jvp(tsh,shp->thp))/dot_general | solution.py:94
  567.2 33.0 %all-gather.18.cloned.1.call-done = bf16[2048,32,128]{2,1,0:T(8,128)(2,1)} async-done(((bf16[128,32,128]{2,1,0:T(8,128)(2,1)}), bf16[2048,32,128]{2,1,0:T(8,128)(2,1)}) %all-gather.18.cloned.1.call-update) | async-done | bytes 16777232 | tf_op jit(solution)/shard_map/all_gather | solution.py:24
  603.0 16.0 %fusion.87 = (f32[128,128]{0,1:T(8,128)S(1)}, f32[128,128]{0,1:T(8,128)S(1)}) fusion(bf16[64,128,32]{0,2,1:T(8,128)(2,1)S(1)} %bitcast.416, bf16[64,128,32]{0,2,1:T(8,128)(2,1)} %bitcast.419, f32[128,32,128]{2,1,0:T(8,128)S(1)} %get-tuple-element.181, f32[128,128,128]{2,0,1:T(8,128)} %bitcast.405), kind=kOutput, calls=%fused_computation.111 | convolution fusion | flops 809467904 | bytes 11665408 | tf_op jit(solution)/shard_map/jvp(hpn,thn->thp)/dot_general | solution.py:96
  625.0 99.0 %psum.7 = f32[2,128]{1,0:T(2,128)} all-reduce(f32[2,128]{1,0:T(2,128)S(1)} %pad_maximum_fusion.3), channel_id=1, replica_groups=mesh['dp'=8,'ctx'=16] {'dp','ctx'}, use_global_device_ids=true, to_apply=%region_39.40 | all-reduce | flops 256 | bytes 2048 | tf_op jit(solution)/shard_map/psum | solution.py:213
  (333 shorter events, 173.1 us)
Async XLA Ops:
  7.2 45.5 %all-gather.12.cloned.1.call-start = ((), (), s32[]{:S(2)}) async-start(), calls=%async_computation.2 | async-start | bytes 2228224 | tf_op jit(solution)/shard_map/all_gather | solution.py:135
  7.9 75.2 %all-gather.14.cloned.1.call-start = ((), (), s32[]{:S(2)}) async-start(), calls=%async_computation.3 | async-start | bytes 2228224 | tf_op jit(solution)/shard_map/all_gather | solution.py:136
  8.7 397.8 %all-gather.16.cloned.1.call-start = ((), (), s32[]{:S(2)}) async-start(), calls=%async_computation.4 | async-start | bytes 35651584 | tf_op jit(solution)/shard_map/all_gather | solution.py:43
  11.1 41.6 %copy-start.22 = (bf16[128,1024]{0,1:T(8,128)(2,1)}, bf16[128,1024]{0,1:T(8,128)(2,1)S(1)}, u32[]{:S(2)}) copy-start(bf16[128,1024]{0,1:T(8,128)(2,1)S(1)} %get-tuple-element.275) | copy-start | bytes 786436
  11.2 44.0 %copy-start.26 = (bf16[128,1024]{0,1:T(8,128)(2,1)}, bf16[128,1024]{0,1:T(8,128)(2,1)S(1)}, u32[]{:S(2)}) copy-start(bf16[128,1024]{0,1:T(8,128)(2,1)S(1)} %get-tuple-element.273) | copy-start | bytes 786436
  16.5 34.4 %copy-start.38 = (bf16[128,1024]{0,1:T(8,128)(2,1)S(1)}, bf16[128,1024]{0,1:T(8,128)(2,1)}, u32[]{:S(2)}) copy-start(bf16[128,1024]{0,1:T(8,128)(2,1)} %get-tuple-element.277) | copy-start | bytes 786436
  16.5 34.4 %copy-start.39 = (bf16[128,1024]{0,1:T(8,128)(2,1)S(1)}, bf16[128,1024]{0,1:T(8,128)(2,1)}, u32[]{:S(2)}) copy-start(bf16[128,1024]{0,1:T(8,128)(2,1)} %get-tuple-element.278) | copy-start | bytes 786436
  16.5 34.4 %copy-start.40 = (bf16[128,1024]{0,1:T(8,128)(2,1)S(1)}, bf16[128,1024]{0,1:T(8,128)(2,1)}, u32[]{:S(2)}) copy-start(bf16[128,1024]{0,1:T(8,128)(2,1)} %get-tuple-element.279) | copy-start | bytes 786436
  52.7 61.7 %copy-start.24 = (pred[128,2048]{0,1:T(8,128)(4,1)}, pred[128,2048]{0,1:T(8,128)(4,1)S(1)}, u32[]{:S(2)}) copy-start(pred[128,2048]{0,1:T(8,128)(4,1)S(1)} %compare_and_fusion) | copy-start | bytes 786436
  79.6 23.0 %copy-start.62 = (f32[8,128]{1,0:T(8,128)}, f32[8,128]{1,0:T(8,128)S(1)}, u32[]{:S(2)}) copy-start(f32[8,128]{1,0:T(8,128)S(1)} %log_add_fusion.2) | copy-start | bytes 12292
  122.8 77.9 %copy-start.71 = (f32[128]{0:T(128)S(1)}, f32[128]{0:T(128)}, u32[]{:S(2)}) copy-start(f32[128]{0:T(128)} %param.26) | copy-start | bytes 1540
  122.8 80.2 %copy-start.30 = (f32[1,128,128]{2,1,0:T(8,128)S(1)}, f32[1,128,128]{2,1,0:T(8,128)}, u32[]{:S(2)}) copy-start(f32[1,128,128]{2,1,0:T(8,128)} %param.25) | copy-start | bytes 196612
  135.7 2.0 collective-permute-start
  137.7 13.3 %collective-permute-start.1 = (bf16[64,4096]{1,0:T(8,128)(2,1)S(1)}, bf16[64,4096]{1,0:T(8,128)(2,1)S(1)}, u32[]{:S(2)}, u32[]{:S(2)}) collective-permute-start(bf16[64,4096]{1,0:T(8,128)(2,1)S(1)} %collective-permute-done), channel_id=1, source_target_pairs={{0,2},{1,3},{2,0},{3,1},{4,6},{5,7},{6,4},{7,5},{8,10},{9,11},{10,... | collective-permute-start | bytes 1572872 | tf_op jit(solution)/shard_map/ppermute | solution.py:18
  150.9 12.3 %collective-permute-start.2 = (bf16[64,4096]{1,0:T(8,128)(2,1)S(1)}, bf16[64,4096]{1,0:T(8,128)(2,1)S(1)}, u32[]{:S(2)}, u32[]{:S(2)}) collective-permute-start(bf16[64,4096]{1,0:T(8,128)(2,1)S(1)} %collective-permute-done.1), channel_id=1, source_target_pairs={{0,4},{1,5},{2,6},{3,7},{4,0},{5,1},{6,2},{7,3},{8,12},{9,13},{10,... | collective-permute-start | bytes 1572872 | tf_op jit(solution)/shard_map/ppermute | solution.py:18
  163.2 12.9 %collective-permute-start.3 = (bf16[64,4096]{1,0:T(8,128)(2,1)S(1)}, bf16[64,4096]{1,0:T(8,128)(2,1)S(1)}, u32[]{:S(2)}, u32[]{:S(2)}) collective-permute-start(bf16[64,4096]{1,0:T(8,128)(2,1)S(1)} %collective-permute-done.2), channel_id=1, source_target_pairs={{0,8},{1,9},{2,10},{3,11},{4,12},{5,13},{6,14},{7,15},{8,0},{9,1},... | collective-permute-start | bytes 1572872 | tf_op jit(solution)/shard_map/ppermute | solution.py:18
  176.2 12.1 %collective-permute-start.4 = (bf16[64,4096]{1,0:T(8,128)(2,1)S(1)}, bf16[64,4096]{1,0:T(8,128)(2,1)S(1)}, u32[]{:S(2)}, u32[]{:S(2)}) collective-permute-start(bf16[64,4096]{1,0:T(8,128)(2,1)S(1)} %broadcast_select_fusion.4), channel_id=1, source_target_pairs={{0,8},{1,9},{2,10},{3,11},{4,12},{5,13},{6,14},{7,15},{8,0},{9,1},... | collective-permute-start | bytes 1572872 | tf_op jit(solution)/shard_map/ppermute | solution.py:18
  189.3 9.8 %collective-permute-start.5 = (bf16[64,4096]{1,0:T(8,128)(2,1)}, bf16[64,4096]{1,0:T(8,128)(2,1)S(1)}, u32[]{:S(2)}, u32[]{:S(2)}) collective-permute-start(bf16[64,4096]{1,0:T(8,128)(2,1)} %get-tuple-element.264), channel_id=1, source_target_pairs={{0,4},{1,5},{2,6},{3,7},{4,0},{5,1},{6,2},{7,3},{8,12},{9,13},{10,... | collective-permute-start | bytes 1572872 | tf_op jit(solution)/shard_map/ppermute | solution.py:18
  200.2 8.7 %collective-permute-start.6 = (bf16[64,4096]{1,0:T(8,128)(2,1)S(1)}, bf16[64,4096]{1,0:T(8,128)(2,1)S(1)}, u32[]{:S(2)}, u32[]{:S(2)}) collective-permute-start(bf16[64,4096]{1,0:T(8,128)(2,1)S(1)} %get-tuple-element.262), channel_id=1, source_target_pairs={{0,2},{1,3},{2,0},{3,1},{4,6},{5,7},{6,4},{7,5},{8,10},{9,11},{10,... | collective-permute-start | bytes 1572872 | tf_op jit(solution)/shard_map/ppermute | solution.py:18
  209.1 10.4 %collective-permute-start.7 = (bf16[64,4096]{1,0:T(8,128)(2,1)S(1)}, bf16[64,4096]{1,0:T(8,128)(2,1)}, u32[]{:S(2)}, u32[]{:S(2)}) collective-permute-start(bf16[64,4096]{1,0:T(8,128)(2,1)S(1)} %broadcast_select_fusion.10), channel_id=1, source_target_pairs={{0,1},{1,0},{2,3},{3,2},{4,5},{5,4},{6,7},{7,6},{8,9},{9,8},{10,11... | collective-permute-start | bytes 1572872 | tf_op jit(solution)/shard_map/ppermute | solution.py:18
  215.5 247.7 %copy-start.58 = (f32[128]{0:T(128)}, f32[128]{0:T(128)S(1)}, u32[]{:S(2)}) copy-start(f32[128]{0:T(128)S(1)} %get-tuple-element.291) | copy-start | bytes 1540
  236.7 312.7 %reduce-scatter.2.cloned.1.call-start = ((), (), s32[]{:S(2)}) async-start(), calls=%async_computation.1 | async-start | bytes 8912896 | tf_op jit(solution)/shard_map/reduce_scatter | solution.py:173
  263.2 337.1 %all-gather.18.cloned.1.call-start = ((), (), s32[]{:S(2)}) async-start(), calls=%async_computation.5 | async-start | bytes 17825792 | tf_op jit(solution)/shard_map/all_gather | solution.py:24
  264.9 35.9 %copy-start.36 = (bf16[128,4,128]{2,1,0:T(4,128)(2,1)}, bf16[128,4,128]{2,1,0:T(4,128)(2,1)S(1)}, u32[]{:S(2)}) copy-start(bf16[128,4,128]{2,1,0:T(4,128)(2,1)S(1)} %reshape_squeeze.7) | copy-start | bytes 393220
  265.0 198.3 %copy-start.56 = (f32[128]{0:T(128)}, f32[128]{0:T(128)S(1)}, u32[]{:S(2)}) copy-start(f32[128]{0:T(128)S(1)} %get-tuple-element.288) | copy-start | bytes 1540
  442.5 34.3 %copy-start.1 = (f32[128,32,128]{2,1,0:T(8,128)}, f32[128,32,128]{2,1,0:T(8,128)S(1)}, u32[]{:S(2)}) copy-start(f32[128,32,128]{2,1,0:T(8,128)S(1)} %get-tuple-element.180) | copy-start | bytes 6291460
  442.5 23.8 %copy-start.67 = (f32[128]{0:T(128)S(1)}, f32[128]{0:T(128)}, u32[]{:S(2)}) copy-start(f32[128]{0:T(128)} %multiply_multiply_fusion.3) | copy-start | bytes 1540
  476.8 29.7 %copy-start.68 = (f32[128]{0:T(128)S(1)}, f32[128]{0:T(128)}, u32[]{:S(2)}) copy-start(f32[128]{0:T(128)} %param.27) | copy-start | bytes 1540
  476.8 30.3 %copy-start.12 = (bf16[64,4096]{1,0:T(8,128)(2,1)S(1)}, bf16[64,4096]{1,0:T(8,128)(2,1)}, u32[]{:S(2)}) copy-start(bf16[64,4096]{1,0:T(8,128)(2,1)} %copy-done.11) | copy-start | bytes 1572868
  476.8 30.3 %copy-start.14 = (bf16[64,4096]{1,0:T(8,128)(2,1)S(1)}, bf16[64,4096]{1,0:T(8,128)(2,1)}, u32[]{:S(2)}) copy-start(bf16[64,4096]{1,0:T(8,128)(2,1)} %copy-done.13) | copy-start | bytes 1572868
  477.0 30.0 %copy-start.37 = (f32[128,128]{0,1:T(8,128)}, f32[128,128]{0,1:T(8,128)S(1)}, u32[]{:S(2)}) copy-start(f32[128,128]{0,1:T(8,128)S(1)} %copy.153) | copy-start | bytes 196612
  532.5 22.0 %copy-start.70 = (f32[128]{0:T(128)S(1)}, f32[128]{0:T(128)}, u32[]{:S(2)}) copy-start(f32[128]{0:T(128)} %broadcast_multiply_fusion) | copy-start | bytes 1540
  (61 other events, 565.9 us)
Sparse Core Ops, SparseCore 0:
  9.7 37.6 all-gather.11
  49.1 33.9 all-gather.13
  236.8 169.5 all-gather.15
  408.7 97.1 reduce-scatter.1
  507.5 92.7 all-gather.17
where the time goes:
time: 742 us; the launch traced here: 731 us
  waiting for transfers between devices  205 us (28%)
  matrix products  182 us (25%)
  blocking collectives  156 us (21%)
  other arithmetic  78.9 us (11%)
  local copies, waits for them, and re-layouts  78 us (11%)
  between operations  16.7 us (2%)
  starting transfers between devices  13 us (2%)
    all_gather x1, waiting for transfers between devices, entering_2(): everything = jax.tree.map(lambda part: lax.all_gather(part, axis), array)  106 us
    psum x1, blocking collectives, shards(): lax.psum(jnp.stack([grad_a1 + grad_a2, grad_s1 + grad_s2]), ('dp', 'ctx'))  99 us
    ppermute x8, waiting for transfers between devices, partner(): lax.ppermute(array, axis, [(i, i ^ 1 << bit) for i in range(lax.axis_size...  61.9 us
    dot_general x3, matrix products, ssd_span(): jnp.einsum('shp,shn->hpn', (tail * step)[:, :, None] * xheads, bheads, pr...  43 us
    dot_general x4, matrix products, ssd_span(): intra = jnp.einsum('tsh,shp->thp', weights, xheads, precision=HIGHEST)  35.5 us
    select_n x16, other arithmetic, step(): return jax.tree.map(lambda a, b: jnp.where(reached, a, b), new, before)  35.1 us
    all_gather x1, waiting for transfers between devices, carried_in(): lax.all_gather(a.astype(kind), axis)  33 us
    unnamed x168, local copies, waits for them, and re-layouts  27.9 us
  transfers between devices with their start and end apart: 13, of which 10 were waited for; matrix products, arithmetic and copies ran while one was open for 33% of the time, Pallas kernels for 0%

commit v1 on v0

v1 whole, which is shorter than its diff:
```python
import functools

import jax
import jax.numpy as jnp
from jax import lax
from jax.experimental import pallas as pl
from jax.experimental.pallas import tpu as pltpu
from jax.sharding import PartitionSpec as P

QHEADS = 32
KVHEADS = 4
HEAD_DIM = 128
SSM_HEADS = 128
SSM_DIM = 32
STATE = 128
SEQ = 2048
ROWS = 128
HALF = 64
CTX = 16
DP = 8
WIDTH = 256
OWN = 8
BLOCK = 256
SPAN = 5
SCALE = HEAD_DIM ** (-0.5)
FAR = -1e30

MESH = pl.DeviceIdType.MESH
HIGHEST = lax.Precision.HIGHEST
F32 = jnp.float32
BF16 = jnp.bfloat16


def dot(a, b, dims, precision=None):
    return lax.dot_general(a, b, (dims, ((), ())), precision=precision, preferred_element_type=F32)


NN = ((1,), (0,))
NT = ((1,), (1,))
TN = ((0,), (0,))


def three(a):
    high = a.astype(BF16)
    rest = a - high.astype(F32)
    mid = rest.astype(BF16)
    low = (rest - mid.astype(F32)).astype(BF16)
    return high, mid, low


def greet(axis, count):
    me = lax.axis_index(axis)
    barrier = pltpu.get_barrier_semaphore()

    def one(off, _):
        pl.semaphore_signal(barrier, inc=1, device_id={axis: lax.rem(me + off, count)}, device_id_type=MESH)
        return 0

    lax.fori_loop(1, count, one, 0)


def await_greetings(total):
    pl.semaphore_wait(pltpu.get_barrier_semaphore(), total)


def pack_small(out_grad, saved, ids, step, alog, small):
    ones = jnp.ones((8, HEAD_DIM), F32)
    sub = lax.broadcasted_iota(jnp.int32, (8, ROWS), 0)
    docs = jnp.broadcast_to(ids[...].astype(F32), (8, ROWS))
    rate = step[0] * -jnp.exp(alog[...])
    upto = lax.broadcasted_iota(jnp.int32, (ROWS, ROWS), 0) <= lax.broadcasted_iota(jnp.int32, (ROWS, ROWS), 1)
    totals = dot(rate, upto.astype(F32), TN, HIGHEST)
    steps = step[0].T
    for j in range(CTX):
        small[j, 0:8, :] = steps[8 * j : 8 * j + 8]
        small[j, 8:16, :] = totals[8 * j : 8 * j + 8]

    def one(j, _):
        deltas = []
        for h in range(2):
            cols = pl.ds(pl.multiple_of(WIDTH * j + HEAD_DIM * h, HEAD_DIM), HEAD_DIM)
            product = out_grad[0, :, cols].astype(F32) * saved[0, :, cols].astype(F32)
            deltas.append(dot(ones, product, NT, HIGHEST))
        small[j, 16:24, :] = jnp.where(sub == 0, deltas[0], jnp.where(sub == 1, deltas[1], docs))
        return 0

    lax.fori_loop(0, CTX, one, 0)


def in_moves(peer, place, arrays, landed):
    q, d, k, v, x, b, c, small = arrays
    lq, ld, lk, lv, lx, lb, lc, ls = landed
    wide = pl.ds(pl.multiple_of(peer * WIDTH, WIDTH), WIDTH)
    narrow = pl.ds(pl.multiple_of(peer // 4 * HEAD_DIM, HEAD_DIM), HEAD_DIM)
    early = pl.ds(pl.multiple_of(place * HALF, HALF), HALF)
    late = pl.ds(pl.multiple_of((2 * CTX - 1 - place) * HALF, HALF), HALF)
    here = pl.ds(pl.multiple_of(place * ROWS, ROWS), ROWS)
    first, second = pl.ds(0, HALF), pl.ds(HALF, HALF)
    moves = []
    for src, dst in ((k, lk), (v, lv)):
        moves.append((src.at[0, second, narrow], dst.at[late, :]))
        moves.append((src.at[0, first, narrow], dst.at[early, :]))
    for src, dst in ((q, lq), (d, ld)):
        moves.append((src.at[0, second, wide], dst.at[late, :]))
    for src, dst in ((q, lq), (d, ld)):
        moves.append((src.at[0, first, wide], dst.at[early, :]))
    for src, dst in ((b, lb), (c, lc)):
        moves.append((src.at[0, :, narrow], dst.at[here, :]))
    moves.append((x.at[0, :, wide], lx.at[here, :]))
    moves.append((small.at[peer], ls.at[place]))
    return moves


KINDS = 12


def in_kernel(q, d, k, v, x, b, c, dv, o, ids, step, alog, *rest):
    landed = rest[:8]
    small, send_sem, recv_sem, own_sem = rest[8:]
    me = lax.axis_index("ctx")
    arrays = (q, d, k, v, x, b, c, small)

    def remote(kind, to, frm):
        src, dst = in_moves(to, frm, arrays, landed)[kind]
        return src, dst

    def send(off, kinds):
        to = lax.rem(me + off, CTX)
        for kind in kinds:
            src, dst = remote(kind, to, me)
            pltpu.make_async_remote_copy(
                src_ref=src, dst_ref=dst, send_sem=send_sem.at[kind, to], recv_sem=recv_sem.at[kind, me],
                device_id={"ctx": to}, device_id_type=MESH,
            ).start()

    greet("ctx", CTX)
    await_greetings(CTX - 1)
    bulk = tuple(range(KINDS - 1))
    for kinds in (bulk,):
        lax.fori_loop(1, CTX, lambda off, _: (send(off, kinds), 0)[1], 0)
    for kind in bulk:
        src, dst = remote(kind, me, me)
        pltpu.make_async_copy(src, dst, own_sem.at[kind]).start()
    pack_small(dv, o, ids, step, alog, small)
    lax.fori_loop(1, CTX, lambda off, _: (send(off, (KINDS - 1,)), 0)[1], 0)
    src, dst = remote(KINDS - 1, me, me)
    pltpu.make_async_copy(src, dst, own_sem.at[KINDS - 1]).start()

    def finish(off, _):
        to = lax.rem(me + off, CTX)
        frm = lax.rem(me + CTX - off, CTX)
        for kind in range(KINDS):
            src, dst = remote(kind, to, frm)
            copy = pltpu.make_async_remote_copy(
                src_ref=src, dst_ref=dst, send_sem=send_sem.at[kind, to], recv_sem=recv_sem.at[kind, frm],
                device_id={"ctx": to}, device_id_type=MESH,
            )
            copy.wait_send()
            copy.wait_recv()
        return 0

    lax.fori_loop(1, CTX, finish, 0)
    for kind in range(KINDS):
        src, dst = remote(kind, me, me)
        pltpu.make_async_copy(src, dst, own_sem.at[kind]).wait()


def exchange_in(q, k, v, o, d, ids, x, b, c, step, alog):
    hbm = pl.BlockSpec(memory_space=pl.ANY)
    vmem = pl.BlockSpec(memory_space=pltpu.VMEM)
    shapes = (
        [jax.ShapeDtypeStruct((SEQ, WIDTH), BF16)] * 2
        + [jax.ShapeDtypeStruct((SEQ, HEAD_DIM), BF16)] * 2
        + [jax.ShapeDtypeStruct((SEQ, WIDTH), BF16)]
        + [jax.ShapeDtypeStruct((SEQ, STATE), BF16)] * 2
        + [jax.ShapeDtypeStruct((CTX, 24, ROWS), F32)]
    )
    return pl.pallas_call(
        in_kernel,
        out_shape=shapes,
        in_specs=[hbm] * 7 + [vmem] * 5,
        out_specs=[hbm] * 8,
        scratch_shapes=[
            pltpu.VMEM((CTX, 24, ROWS), F32),
            pltpu.SemaphoreType.DMA((KINDS, CTX)),
            pltpu.SemaphoreType.DMA((KINDS, CTX)),
            pltpu.SemaphoreType.DMA((KINDS,)),
        ],
        compiler_params=pltpu.CompilerParams(
            collective_id=0, has_side_effects=True, vmem_limit_bytes=32 * 2**20
        ),
        name="exchange_in",
    )(q, d, k, v, x, b, c, d, o, ids, step, alog)


def spread_columns(small, dcol, doccol):
    row = lax.broadcasted_iota(jnp.int32, (24, 3 * ROWS), 0) % 8
    lane = lax.broadcasted_iota(jnp.int32, (24, 3 * ROWS), 1) // ROWS
    pick = jnp.where(row == lane, 1.0, 0.0).astype(BF16)
    doccol[0:8, :] = jnp.full((8, ROWS), -1.0, F32)

    def one(src, _):
        parts = jnp.concatenate([p.astype(F32) for p in three(small[src, 16:24, :])], axis=0).astype(BF16)
        wide = dot(parts, pick, TN)
        early = pl.multiple_of(src * HALF, HALF)
        late = pl.multiple_of((2 * CTX - 1 - src) * HALF, HALF)
        dcol[pl.ds(early, HALF), :] = wide[:HALF, : 2 * ROWS]
        dcol[pl.ds(late, HALF), :] = wide[HALF:, : 2 * ROWS]
        doccol[pl.ds(pl.multiple_of(8 + src * ROWS, 8), ROWS), :] = wide[:, 2 * ROWS :]
        return 0

    lax.fori_loop(0, CTX, one, 0)


def attention_block(i, q, d, k, v, small, dcol, doccol, dk, dv, cot, q2, d2, s_ref, m_ref, l_ref, dq):
    base = pl.multiple_of(i * BLOCK, BLOCK)
    rows = pl.ds(base, BLOCK)
    q2[:BLOCK, :] = q[rows, :HEAD_DIM]
    q2[BLOCK:, :] = q[rows, HEAD_DIM:]
    d2[:BLOCK, :] = d[rows, :HEAD_DIM]
    d2[BLOCK:, :] = d[rows, HEAD_DIM:]
    m_ref[...] = jnp.full(m_ref.shape, FAR, F32)
    l_ref[...] = jnp.zeros(l_ref.shape, F32)
    dq[...] = jnp.zeros(dq.shape, F32)
    first = jnp.maximum(i - (SPAN - 1), 0)
    ahead = lax.broadcasted_iota(jnp.int32, (BLOCK, BLOCK), 0) - lax.broadcasted_iota(jnp.int32, (BLOCK, BLOCK), 1)

    def scores(j, _):
        keys = k[pl.ds(pl.multiple_of(j * BLOCK, BLOCK), BLOCK), :]
        own = doccol[pl.ds(pl.multiple_of(8 + base, 8), BLOCK), :]
        own = jnp.concatenate([own, own], axis=1)
        theirs = jnp.concatenate([small[2 * j, 18:19, :], small[2 * j + 1, 18:19, :]], axis=1)
        allowed = (own == theirs) & (ahead >= (j - i) * BLOCK)
        for h in range(2):
            part = pl.ds(h * BLOCK, BLOCK)
            s = jnp.where(allowed, dot(q2[part, :], keys, NT), FAR)
            s_ref[j - first, part, :] = s
            m_ref[part, :] = jnp.maximum(m_ref[part, :], jnp.maximum(s[:, :ROWS], s[:, ROWS:]))
        return 0

    lax.fori_loop(first, i + 1, scores, 0)
    m_ref[...] = jnp.broadcast_to(jnp.max(m_ref[...], axis=1, keepdims=True), m_ref.shape)

    def exps(j, _):
        for h in range(2):
            part = pl.ds(h * BLOCK, BLOCK)
            m = m_ref[part, :]
            e = jnp.exp((s_ref[j - first, part, :] - jnp.concatenate([m, m], axis=1)) * SCALE)
            s_ref[j - first, part, :] = e
            l_ref[part, :] += e[:, :ROWS] + e[:, ROWS:]
        return 0

    lax.fori_loop(first, i + 1, exps, 0)
    l_ref[...] = jnp.broadcast_to(1.0 / jnp.sum(l_ref[...], axis=1, keepdims=True), l_ref.shape)

    def grads(j, _):
        there = pl.ds(pl.multiple_of(j * BLOCK, BLOCK), BLOCK)
        keys, vals = k[there, :], v[there, :]
        probs, scaled = [], []
        for h in range(2):
            part = pl.ds(h * BLOCK, BLOCK)
            inv = l_ref[part, :]
            p = s_ref[j - first, part, :] * jnp.concatenate([inv, inv], axis=1)
            delta = dcol[rows, h * ROWS : (h + 1) * ROWS]
            dp = dot(d2[part, :], vals, NT) - jnp.concatenate([delta, delta], axis=1)
            ds = (p * dp * SCALE).astype(BF16)
            dq[part, :] += dot(ds, keys, NN)
            probs.append(p.astype(BF16))
            scaled.append(ds)
        dk[there, :] += dot(jnp.concatenate(scaled, axis=0), q2[...], TN)
        dv[there, :] += dot(jnp.concatenate(probs, axis=0), d2[...], TN)
        return 0

    lax.fori_loop(first, i + 1, grads, 0)
    cot[:, :HEAD_DIM] = dq[:BLOCK, :].astype(BF16)
    cot[:, HEAD_DIM:] = dq[BLOCK:, :].astype(BF16)


def spread_matrix(spread):
    row = lax.broadcasted_iota(jnp.int32, spread.shape, 0)
    lane = lax.broadcasted_iota(jnp.int32, spread.shape, 1)
    head = row % OWN
    a = (lane < 1024) & (row < 24) & (lane // ROWS == head)
    b = (lane >= 1024) & (lane < 1280) & (row < 24) & ((lane - 1024) // SSM_DIM == head)
    c = (lane >= 1280) & (row >= 24) & ((lane - 1280) // SSM_DIM == head)
    spread[...] = jnp.where(a | b | c, 1.0, 0.0).astype(BF16)


def ssm_chunk(c, at, x, b, cm, small, doccol, cot, skip, spread, gstate, gtimed, acc_a, acc_s, dx):
    base = pl.multiple_of(c * ROWS, ROWS)
    here = pl.ds(base, ROWS)
    bc, cc = b[here, :], cm[here, :]
    xc = x[here, :].astype(F32)
    dyb = cot[at : at + ROWS, :]
    dy = dyb.astype(F32)
    steps, totals = small[c, 0:8, :], small[c, 8:16, :]
    parts = jnp.concatenate([p.astype(F32) for p in three(totals) + three(steps)], axis=0).astype(BF16)
    wide = dot(parts, spread[...], TN)
    te, se = wide[:, 1024:1280], wide[:, 1280:1536]
    docs = doccol[pl.ds(pl.multiple_of(8 + base, 8), ROWS), :]
    before = doccol[pl.ds(7 + base, 1), :]
    last = doccol[pl.ds(7 + ROWS + base, 1), :]
    docrow = small[c, 18:19, :]
    sub = lax.broadcasted_iota(jnp.int32, (ROWS, ROWS), 0)
    lane = lax.broadcasted_iota(jnp.int32, (ROWS, ROWS), 1)
    inner = jnp.where((sub <= lane) & (docs == docrow), dot(bc, cc, NT), 0.0)

    plain, timed = [], []
    for half in range(2):
        dyh = dyb[:, half * 128 : half * 128 + 128]
        total = None
        for pair in range(2):
            tops, lows, rights = [], [], []
            for one in range(2):
                local = 2 * pair + one
                h = 4 * half + local
                gap = totals[h : h + 1, :] - wide[:, ROWS * h : ROWS * h + ROWS]
                w = inner * jnp.exp(gap)
                tops.append(w.astype(BF16))
                lows.append((w * gap).astype(BF16))
                rights.append(jnp.where(lane // SSM_DIM == local, dyh.astype(F32), 0.0).astype(BF16))
            left = jnp.concatenate([jnp.concatenate(tops, axis=1), jnp.concatenate(lows, axis=1)], axis=0)
            out = dot(left, jnp.concatenate(rights, axis=0), NN)
            total = out if total is None else total + out
        plain.append(total[:ROWS])
        timed.append(total[ROWS:])
    intra = jnp.concatenate(plain, axis=1)
    intra_t = jnp.concatenate(timed, axis=1)

    both = jnp.concatenate([gstate[...], gtimed[...]], axis=1).astype(BF16)
    inter = dot(bc, both, NN)
    te_last = te[ROWS - 1 : ROWS, :]
    docs2 = jnp.concatenate([docs, docs], axis=1)
    before2 = jnp.concatenate([before, before], axis=1)
    last2 = jnp.concatenate([last, last], axis=1)
    left_time = te_last - te
    leave = jnp.where(docs2 == last2, jnp.exp(left_time), 0.0)
    got = intra + leave * inter[:, :WIDTH]
    got_t = intra_t + leave * (left_time * inter[:, :WIDTH] + inter[:, WIDTH:])
    dx[here, :] = (se * got + skip[...] * dy).astype(BF16)
    acc_a[...] += se * xc * got_t
    acc_s[...] += dy * xc

    enter = jnp.where(docs2 == before2, jnp.exp(te), 0.0)
    dye = dy * enter
    fresh = dot(cc, jnp.concatenate([dye, dye * te], axis=1).astype(BF16), TN)
    whole = jnp.where(last2 == before2, jnp.exp(te_last), 0.0)
    old = gstate[...]
    gtimed[...] = whole * (gtimed[...] + te_last * old) + fresh[:, WIDTH:]
    gstate[...] = whole * old + fresh[:, :WIDTH]


def finish_decay(me, acc_a, acc_s):
    sums = jnp.concatenate(
        [jnp.sum(acc_a[...], axis=0, keepdims=True), jnp.sum(acc_s[...], axis=0, keepdims=True), jnp.zeros((6, WIDTH), F32)],
        axis=0,
    )
    lane = lax.broadcasted_iota(jnp.int32, (WIDTH, SSM_HEADS), 0)
    head = lax.broadcasted_iota(jnp.int32, (WIDTH, SSM_HEADS), 1)
    place = jnp.where(lane // SSM_DIM + me * OWN == head, 1.0, 0.0)
    return dot(sums, place, NN, HIGHEST)


def compute_kernel(q, d, k, v, x, b, c, small, skip, dx, gk, gv, decay,
                   dk, dv, cot, q2, d2, s_ref, m_ref, l_ref, dq, dcol, doccol, spread, gstate, gtimed, acc_a, acc_s):
    me = lax.axis_index("ctx")
    for ref in (dk, dv, gstate, gtimed, acc_a, acc_s):
        ref[...] = jnp.zeros(ref.shape, F32)
    spread_columns(small, dcol, doccol)
    spread_matrix(spread)

    def step(n, _):
        i = SEQ // BLOCK - 1 - n
        attention_block(i, q, d, k, v, small, dcol, doccol, dk, dv, cot, q2, d2, s_ref, m_ref, l_ref, dq)
        for sub in (1, 0):
            ssm_chunk(2 * i + sub, sub * ROWS, x, b, c, small, doccol, cot, skip, spread, gstate, gtimed, acc_a, acc_s, dx)
        return 0

    lax.fori_loop(0, SEQ // BLOCK, step, 0)
    gk[...] = dk[...].astype(BF16)
    gv[...] = dv[...].astype(BF16)
    decay[...] = finish_decay(me, acc_a, acc_s)


COMPUTE_SCRATCH = [
    pltpu.VMEM((SEQ, HEAD_DIM), F32),
    pltpu.VMEM((SEQ, HEAD_DIM), F32),
    pltpu.VMEM((BLOCK, WIDTH), BF16),
    pltpu.VMEM((2 * BLOCK, HEAD_DIM), BF16),
    pltpu.VMEM((2 * BLOCK, HEAD_DIM), BF16),
    pltpu.VMEM((SPAN, 2 * BLOCK, BLOCK), F32),
    pltpu.VMEM((2 * BLOCK, ROWS), F32),
    pltpu.VMEM((2 * BLOCK, ROWS), F32),
    pltpu.VMEM((2 * BLOCK, HEAD_DIM), F32),
    pltpu.VMEM((SEQ, 2 * ROWS), F32),
    pltpu.VMEM((SEQ + 8, ROWS), F32),
    pltpu.VMEM((48, 1536), BF16),
    pltpu.VMEM((STATE, WIDTH), F32),
    pltpu.VMEM((STATE, WIDTH), F32),
    pltpu.VMEM((ROWS, WIDTH), F32),
    pltpu.VMEM((ROWS, WIDTH), F32),
]


def compute(q, d, k, v, x, b, c, small, skip):
    vmem = pl.BlockSpec(memory_space=pltpu.VMEM)
    return pl.pallas_call(
        compute_kernel,
        out_shape=[
            jax.ShapeDtypeStruct((SEQ, WIDTH), BF16),
            jax.ShapeDtypeStruct((SEQ, HEAD_DIM), BF16),
            jax.ShapeDtypeStruct((SEQ, HEAD_DIM), BF16),
            jax.ShapeDtypeStruct((8, SSM_HEADS), F32),
        ],
        in_specs=[vmem] * 9,
        out_specs=[vmem] * 4,
        scratch_shapes=COMPUTE_SCRATCH,
        compiler_params=pltpu.CompilerParams(vmem_limit_bytes=48 * 2**20),
        name="head_gradients",
    )(q, d, k, v, x, b, c, small, skip)


def out_moves(peer, place, arrays, landed):
    dx, gk, gv, decay = arrays
    lx, lk, lv, ld = landed
    early = pl.ds(pl.multiple_of(peer * HALF, HALF), HALF)
    late = pl.ds(pl.multiple_of((2 * CTX - 1 - peer) * HALF, HALF), HALF)
    here = pl.ds(pl.multiple_of(peer * ROWS, ROWS), ROWS)
    wide = pl.ds(pl.multiple_of(place * WIDTH, WIDTH), WIDTH)
    first, second = pl.ds(0, HALF), pl.ds(HALF, HALF)
    moves = []
    for src, dst in ((gk, lk), (gv, lv)):
        moves.append((src.at[late, :], dst.at[place, second, :]))
        moves.append((src.at[early, :], dst.at[place, first, :]))
    moves.append((dx.at[here, :], lx.at[0, :, wide]))
    moves.append((decay, ld.at[place]))
    return moves


OUT_KINDS = 6


def out_kernel(dx, gk, gv, decay, grad_x, grad_k, grad_v, grad_d,
               lk, lv, ld, seq_decay, all_decay, send_sem, recv_sem, own_sem, dp_send, dp_recv, dp_own):
    me = lax.axis_index("ctx")
    row = lax.axis_index("dp")
    arrays, landed = (dx, gk, gv, decay), (grad_x, lk, lv, ld)
    greet("ctx", CTX)
    greet("dp", DP)
    await_greetings(CTX - 1 + DP - 1)

    def send(off, _):
        to = lax.rem(me + off, CTX)
        for kind, (src, dst) in enumerate(out_moves(to, me, arrays, landed)):
            pltpu.make_async_remote_copy(
                src_ref=src, dst_ref=dst, send_sem=send_sem.at[kind, to], recv_sem=recv_sem.at[kind, me],
                device_id={"ctx": to}, device_id_type=MESH,
            ).start()
        return 0

    lax.fori_loop(1, CTX, send, 0)
    own = [pltpu.make_async_copy(src, dst, own_sem.at[kind])
           for kind, (src, dst) in enumerate(out_moves(me, me, arrays, landed))]
    for copy in own:
        copy.start()

    def finish(off, kinds):
        to = lax.rem(me + off, CTX)
        frm = lax.rem(me + CTX - off, CTX)
        gone = out_moves(to, me, arrays, landed)
        come = out_moves(me, frm, arrays, landed)
        for kind in kinds:
            pltpu.make_async_remote_copy(
                src_ref=gone[kind][0], dst_ref=gone[kind][1], send_sem=send_sem.at[kind, to],
                recv_sem=recv_sem.at[kind, frm], device_id={"ctx": to}, device_id_type=MESH,
            ).wait_send()
            pltpu.make_async_remote_copy(
                src_ref=come[kind][0], dst_ref=come[kind][1], send_sem=send_sem.at[kind, to],
                recv_sem=recv_sem.at[kind, frm], device_id={"ctx": to}, device_id_type=MESH,
            ).wait_recv()

    lax.fori_loop(1, CTX, lambda off, _: (finish(off, (5,)), 0)[1], 0)
    own[5].wait()
    seq_decay[...] = jnp.sum(ld[...], axis=0)

    def dp_copy(to, frm):
        return pltpu.make_async_remote_copy(
            src_ref=seq_decay, dst_ref=all_decay.at[frm], send_sem=dp_send.at[to], recv_sem=dp_recv.at[frm],
            device_id={"dp": to}, device_id_type=MESH,
        )

    lax.fori_loop(1, DP, lambda off, _: (dp_copy(lax.rem(row + off, DP), row).start(), 0)[1], 0)
    mine = pltpu.make_async_copy(seq_decay, all_decay.at[row], dp_own)
    mine.start()

    lax.fori_loop(1, CTX, lambda off, _: (finish(off, (0, 1, 2, 3, 4)), 0)[1], 0)
    for copy in own[:5]:
        copy.wait()
    for group in range(KVHEADS):
        cols = pl.ds(group * HEAD_DIM, HEAD_DIM)
        for src, dst in ((lk, grad_k), (lv, grad_v)):
            total = src[4 * group].astype(F32)
            for other in range(1, 4):
                total += src[4 * group + other].astype(F32)
            dst[0, :, cols] = total.astype(BF16)

    def dp_finish(off, _):
        copy = dp_copy(lax.rem(row + off, DP), lax.rem(row + DP - off, DP))
        copy.wait_send()
        copy.wait_recv()
        return 0

    lax.fori_loop(1, DP, dp_finish, 0)
    mine.wait()
    total = all_decay[0]
    for other in range(1, DP):
        total += all_decay[other]
    grad_d[...] = total[:2]


def exchange_out(dx, gk, gv, decay):
    hbm = pl.BlockSpec(memory_space=pl.ANY)
    vmem = pl.BlockSpec(memory_space=pltpu.VMEM)
    return pl.pallas_call(
        out_kernel,
        out_shape=[
            jax.ShapeDtypeStruct((1, ROWS, SSM_HEADS * SSM_DIM), BF16),
            jax.ShapeDtypeStruct((1, ROWS, KVHEADS * HEAD_DIM), BF16),
            jax.ShapeDtypeStruct((1, ROWS, KVHEADS * HEAD_DIM), BF16),
            jax.ShapeDtypeStruct((2, SSM_HEADS), F32),
        ],
        in_specs=[hbm] * 4,
        out_specs=[hbm, vmem, vmem, vmem],
        scratch_shapes=[
            pltpu.VMEM((CTX, ROWS, HEAD_DIM), BF16),
            pltpu.VMEM((CTX, ROWS, HEAD_DIM), BF16),
            pltpu.VMEM((CTX, 8, SSM_HEADS), F32),
            pltpu.VMEM((8, SSM_HEADS), F32),
            pltpu.VMEM((DP, 8, SSM_HEADS), F32),
            pltpu.SemaphoreType.DMA((OUT_KINDS, CTX)),
            pltpu.SemaphoreType.DMA((OUT_KINDS, CTX)),
            pltpu.SemaphoreType.DMA((OUT_KINDS,)),
            pltpu.SemaphoreType.DMA((DP,)),
            pltpu.SemaphoreType.DMA((DP,)),
            pltpu.SemaphoreType.DMA,
        ],
        compiler_params=pltpu.CompilerParams(
            collective_id=1, has_side_effects=True, vmem_limit_bytes=32 * 2**20
        ),
        name="exchange_out",
    )(dx, gk, gv, decay)


def shards(queries, keys, values, saved, out_grad, doc_ids, inputs, bmat, cmat, step, alog, skip):
    device = lax.axis_index("ctx")
    own_skip = jnp.repeat(lax.dynamic_slice_in_dim(skip, device * OWN, OWN), SSM_DIM)[None]
    landed = exchange_in(queries, keys, values, saved, out_grad, doc_ids, inputs, bmat, cmat, step, alog[None])
    dx, gk, gv, decay = compute(*landed, own_skip)
    grad_x, grad_k, grad_v, grad_d = exchange_out(dx, gk, gv, decay)
    return (grad_k, grad_v, grad_x, grad_d)


def solution(mesh):
    return jax.shard_map(
        shards,
        mesh=mesh,
        in_specs=(
            P("dp", "ctx", None),
            P("dp", "ctx", None),
            P("dp", "ctx", None),
            P("dp", "ctx", None),
            P("dp", "ctx", None),
            P("dp", "ctx"),
            P("dp", "ctx", None),
            P("dp", "ctx", None),
            P("dp", "ctx", None),
            P("dp", "ctx", None),
            P(),
            P(),
        ),
        out_specs=(P("dp", "ctx", None), P("dp", "ctx", None), P("dp", "ctx", None), P()),
        check_vma=False,
    )
```

time: 742 us -> 213 us (0.29); the launches traced: 731 us -> 210 us
  waiting for transfers between devices: 205 us -> 0 us
  Pallas kernels: 0 us -> 194 us
  matrix products: 182 us -> 0 us
  blocking collectives: 156 us -> 0 us
  other arithmetic: 78.9 us -> 0 us
  local copies, waits for them, and re-layouts: 78 us -> 15.6 us
  between operations: 16.7 us -> 0.69 us
  starting transfers between devices: 13 us -> 0 us
    pallas_call x0 -> x3, Pallas kernels: none -> 194 us  [the longest x1 90.3 us: exchange_in(): pl.pallas_call(in_kernel, out_shape=shapes, in_specs=[hbm] * 7 + [vmem] *...]
    dot_general x30 -> x0, matrix products: 182 us -> none  [the longest x3 43 us: ssd_span(): jnp.einsum('shp,shn->hpn', (tail * step)[:, :, None] * xheads, bheads, pr...]
    all_gather x4 -> x0, waiting for transfers between devices: 142 us -> none  [the longest x1 106 us: entering_2(): everything = jax.tree.map(lambda part: lax.all_gather(part, axis), array)]
    psum x1 -> x0, blocking collectives: 99 us -> none  [shards(): lax.psum(jnp.stack([grad_a1 + grad_a2, grad_s1 + grad_s2]), ('dp', 'ctx'))]
    ppermute x8 -> x0, waiting for transfers between devices: 61.9 us -> none  [partner(): lax.ppermute(array, axis, [(i, i ^ 1 << bit) for i in range(lax.axis_size...]
    all_gather x3 -> x0, blocking collectives: 57.2 us -> none  [the longest x1 21.4 us: shards(): lax.all_gather(ids_local, 'ctx', axis=0, tiled=True)]
    select_n x28 -> x0, other arithmetic: 38.8 us -> none  [the longest x16 35.1 us: step(): return jax.tree.map(lambda a, b: jnp.where(reached, a, b), new, before)]
    reduce_sum x9 -> x0, other arithmetic: 24.1 us -> none  [the longest x1 13 us: ssd_span(): diff = total[:, None, :] - total[None, :, :]]
  transfers between devices with their start and end apart: 13 -> 0, of which waited for: 10 -> 0; matrix products, arithmetic and copies ran while one was open for 33% -> 0% of each run, Pallas kernels for 0% -> 0%
where the time goes in v1:
time: 213 us; the launch traced here: 210 us
  Pallas kernels  194 us (91%)
  local copies, waits for them, and re-layouts  15.6 us (7%)
    pallas_call x1, Pallas kernels, exchange_in(): pl.pallas_call(in_kernel, out_shape=shapes, in_specs=[hbm] * 7 + [vmem] *...  90.3 us
    pallas_call x1, Pallas kernels, exchange_out(): pl.pallas_call(out_kernel, out_shape=[jax.ShapeDtypeStruct((1, ROWS, SSM_...  53.5 us
    pallas_call x1, Pallas kernels, compute(): pl.pallas_call(compute_kernel, out_shape=[jax.ShapeDtypeStruct((SEQ, WIDT...  50.2 us
    unnamed x32, local copies, waits for them, and re-layouts  15.4 us

profile of v1, /device:TPU:1, one launch (start us, length us, event | category | flops | bytes accessed | tf_op | source)
XLA Modules:
  0.0 210.2 jit_solution(15284242557164622475)
XLA Ops:
  0.6 0.0 copy-start.13
  0.6 0.6 copy-done.13
  1.3 0.1 dynamic_slice.3
  1.4 0.1 broadcast_in_dim.7
  1.4 0.0 copy-start.11
  1.4 0.0 copy-start.12
  1.4 0.1 broadcast_in_dim_reshape.3.skip
  1.5 0.6 copy-done.11
  2.1 0.0 copy-done.12
  2.1 0.0 copy-start
  2.1 1.2 copy-done
  3.3 0.0 copy-start.1
  3.3 1.2 copy-done.1
  4.6 0.0 copy-start.2
  4.6 1.2 copy-done.2
  5.8 0.0 copy-start.3
  5.8 1.2 copy-done.3
  7.0 0.9 copy-done.6
  7.9 0.9 copy-done.7
  8.8 0.9 copy-done.8
  9.7 0.9 copy-done.9
  10.6 0.8 copy-done.10
  11.5 90.3 %exchange_in.1 = (bf16[2048,256]{1,0:T(8,128)(2,1)S(1)}, bf16[2048,256]{1,0:T(8,128)(2,1)S(1)}, bf16[2048,128]{1,0:T(8,128)(2,1)S(1)}, bf16[2048,128]{1,0:T(8,12...) custom-call(bf16[1,128,4096]{2,1,0:T(8,128)(2,1)S(1)} %copy-done.1, ...), custom_call_target="tpu_custom_call" | custom-call | tf_op jit(solution)/shard_map/exchange_in/pallas_call | solution.py:178
  101.7 0.0 copy-start.4
  101.7 1.0 copy-done.4
  102.7 1.0 copy-done.5
  103.7 50.2 %head_gradients.1 = (bf16[2048,256]{1,0:T(8,128)(2,1)S(1)}, bf16[2048,128]{1,0:T(8,128)(2,1)S(1)}, bf16[2048,128]{1,0:T(8,128)(2,1)S(1)}, f32[8,128]{1,0:T(8,128)S(1)}) custom-call(bf16[2048,256]{1,0:T(8,128)(2,1)S(1)} %get-tuple-element.20.q, bf16[2048,256]{1,0:T(8,128)(2,1)} %copy-done.4, bf16[2048,128]{1,0:T(8,128)(2,1)S(1)} %get-tuple-element.22.k, ...), custom_call_target="tpu_custom_call" | custom-call | tf_op jit(solution)/shard_map/head_gradients/pallas_call | solution.py:407
  153.9 53.5 %exchange_out.1 = (bf16[1,128,4096]{2,1,0:T(8,128)(2,1)S(1)}, bf16[1,128,512]{2,1,0:T(8,128)(2,1)S(1)}, bf16[1,128,512]{2,1,0:T(8,128)(2,1)S(1)}, f32[2,128]{1,0:T(2,128)S(1)}) custom-call(bf16[2048,256]{1,0:T(8,128)(2,1)S(1)} %get-tuple-element.28.dx, bf16[2048,128]{1,0:T(8,128)(2,1)S(1)} %get-tuple-element.29.gk, ...), custom_call_target="tpu_custom_call" | custom-call | tf_op jit(solution)/shard_map/exchange_out/pallas_call | solution.py:524
  207.4 0.7 copy.20
  208.0 0.7 copy.21
  208.7 1.0 copy.22
  209.6 0.6 copy.23
  (6 shorter events, 0.0 us)
Async XLA Ops:
  0.6 0.7 copy-start.13
  1.4 0.7 copy-start.11
  1.4 0.7 copy-start.12
  2.1 1.2 copy-start
  3.3 1.2 copy-start.1
  4.6 1.2 copy-start.2
  5.8 1.2 copy-start.3
  7.0 0.9 copy-start.6
  7.9 0.9 copy-start.7
  8.8 0.9 copy-start.8
  9.7 0.9 copy-start.9
  10.6 0.8 copy-start.10
  101.7 1.0 copy-start.4
  102.7 1.0 copy-start.5

commit v2 on v1

--- a/solution.py
+++ b/solution.py
@@ -1,5 +1,3 @@
-import functools
-
 import jax
 import jax.numpy as jnp
 from jax import lax
@@ -111,86 +109,12 @@
     return moves
 
 
+KV_KINDS = (0, 1, 2, 3)
+LATE_KINDS = (4, 5)
+EARLY_KINDS = (6, 7)
+SSM_KINDS = (8, 9, 10)
+SMALL_KIND = 11
 KINDS = 12
-
-
-def in_kernel(q, d, k, v, x, b, c, dv, o, ids, step, alog, *rest):
-    landed = rest[:8]
-    small, send_sem, recv_sem, own_sem = rest[8:]
-    me = lax.axis_index("ctx")
-    arrays = (q, d, k, v, x, b, c, small)
-
-    def remote(kind, to, frm):
-        src, dst = in_moves(to, frm, arrays, landed)[kind]
-        return src, dst
-
-    def send(off, kinds):
-        to = lax.rem(me + off, CTX)
-        for kind in kinds:
-            src, dst = remote(kind, to, me)
-            pltpu.make_async_remote_copy(
-                src_ref=src, dst_ref=dst, send_sem=send_sem.at[kind, to], recv_sem=recv_sem.at[kind, me],
-                device_id={"ctx": to}, device_id_type=MESH,
-            ).start()
-
-    greet("ctx", CTX)
-    await_greetings(CTX - 1)
-    bulk = tuple(range(KINDS - 1))
-    for kinds in (bulk,):
-        lax.fori_loop(1, CTX, lambda off, _: (send(off, kinds), 0)[1], 0)
-    for kind in bulk:
-        src, dst = remote(kind, me, me)
-        pltpu.make_async_copy(src, dst, own_sem.at[kind]).start()
-    pack_small(dv, o, ids, step, alog, small)
-    lax.fori_loop(1, CTX, lambda off, _: (send(off, (KINDS - 1,)), 0)[1], 0)
-    src, dst = remote(KINDS - 1, me, me)
-    pltpu.make_async_copy(src, dst, own_sem.at[KINDS - 1]).start()
-
-    def finish(off, _):
-        to = lax.rem(me + off, CTX)
-        frm = lax.rem(me + CTX - off, CTX)
-        for kind in range(KINDS):
-            src, dst = remote(kind, to, frm)
-            copy = pltpu.make_async_remote_copy(
-                src_ref=src, dst_ref=dst, send_sem=send_sem.at[kind, to], recv_sem=recv_sem.at[kind, frm],
-                device_id={"ctx": to}, device_id_type=MESH,
-            )
-            copy.wait_send()
-            copy.wait_recv()
-        return 0
-
-    lax.fori_loop(1, CTX, finish, 0)
-    for kind in range(KINDS):
-        src, dst = remote(kind, me, me)
-        pltpu.make_async_copy(src, dst, own_sem.at[kind]).wait()
-
-
-def exchange_in(q, k, v, o, d, ids, x, b, c, step, alog):
-    hbm = pl.BlockSpec(memory_space=pl.ANY)
-    vmem = pl.BlockSpec(memory_space=pltpu.VMEM)
-    shapes = (
-        [jax.ShapeDtypeStruct((SEQ, WIDTH), BF16)] * 2
-        + [jax.ShapeDtypeStruct((SEQ, HEAD_DIM), BF16)] * 2
-        + [jax.ShapeDtypeStruct((SEQ, WIDTH), BF16)]
-        + [jax.ShapeDtypeStruct((SEQ, STATE), BF16)] * 2
-        + [jax.ShapeDtypeStruct((CTX, 24, ROWS), F32)]
-    )
-    return pl.pallas_call(
-        in_kernel,
-        out_shape=shapes,
-        in_specs=[hbm] * 7 + [vmem] * 5,
-        out_specs=[hbm] * 8,
-        scratch_shapes=[
-            pltpu.VMEM((CTX, 24, ROWS), F32),
-            pltpu.SemaphoreType.DMA((KINDS, CTX)),
-            pltpu.SemaphoreType.DMA((KINDS, CTX)),
-            pltpu.SemaphoreType.DMA((KINDS,)),
-        ],
-        compiler_params=pltpu.CompilerParams(
-            collective_id=0, has_side_effects=True, vmem_limit_bytes=32 * 2**20
-        ),
-        name="exchange_in",
-    )(q, d, k, v, x, b, c, d, o, ids, step, alog)
 
 
 def spread_columns(small, dcol, doccol):
@@ -361,28 +285,275 @@
     return dot(sums, place, NN, HIGHEST)
 
 
-def compute_kernel(q, d, k, v, x, b, c, small, skip, dx, gk, gv, decay,
-                   dk, dv, cot, q2, d2, s_ref, m_ref, l_ref, dq, dcol, doccol, spread, gstate, gtimed, acc_a, acc_s):
+def kernel(q, d, k, v, x, b, c, dvm, o, ids, step, alog, skip,
+           grad_x, grad_k, grad_v, grad_d,
+           lq, ld, lk, lv, lx, lb, lc, ls, small, send_sem, recv_sem, own_sem,
+           dk, dv, cot, q2, d2, s_ref, m_ref, l_ref, dq, dcol, doccol, spread, gstate, gtimed, acc_a, acc_s,
+           dx, stage, terms, kv_send, kv_recv, x_send, x_recv, kv_own, x_own,
+           decay, ctx_decay, seq_decay, all_decay, ctx_send, ctx_recv, ctx_own, dp_send, dp_recv, dp_own):
     me = lax.axis_index("ctx")
+    row = lax.axis_index("dp")
+    arrays = (q, d, k, v, x, b, c, small)
+    landed = (lq, ld, lk, lv, lx, lb, lc, ls)
+
+    def in_copy(kind, to, frm, peer):
+        src, dst = in_moves(to, frm, arrays, landed)[kind]
+        return pltpu.make_async_remote_copy(
+            src_ref=src, dst_ref=dst, send_sem=send_sem.at[kind, peer], recv_sem=recv_sem.at[kind, frm],
+            device_id={"ctx": peer}, device_id_type=MESH,
+        )
+
+    def send(kinds):
+        def one(off, _):
+            to = lax.rem(me + off, CTX)
+            for kind in kinds:
+                in_copy(kind, to, me, to).start()
+            return 0
+
+        lax.fori_loop(1, CTX, one, 0)
+
+    def own(kinds):
+        for kind in kinds:
+            src, dst = in_moves(me, me, arrays, landed)[kind]
+            yield pltpu.make_async_copy(src, dst, own_sem.at[kind])
+
+    def arrived(src, kinds):
+        @pl.when(src != me)
+        def _():
+            for kind in kinds:
+                in_copy(kind, me, src, src).wait_recv()
+
+    greet("ctx", CTX)
+    greet("dp", DP)
+    await_greetings(CTX - 1 + DP - 1)
+    send(KV_KINDS)
+    for copy in own(range(KINDS - 1)):
+        copy.start()
+    pack_small(dvm, o, ids, step, alog, small)
+    send((SMALL_KIND,))
+    for copy in own((SMALL_KIND,)):
+        copy.start()
+    send(LATE_KINDS)
+
+    @pl.when(me >= CTX // 2)
+    def _():
+        send(SSM_KINDS)
+
+    send(EARLY_KINDS)
+
+    @pl.when(me < CTX // 2)
+    def _():
+        send(SSM_KINDS)
+
     for ref in (dk, dv, gstate, gtimed, acc_a, acc_s):
         ref[...] = jnp.zeros(ref.shape, F32)
-    spread_columns(small, dcol, doccol)
     spread_matrix(spread)
-
-    def step(n, _):
+    for copy in own(range(KINDS)):
+        copy.wait()
+
+    def first(src, _):
+        arrived(src, KV_KINDS + (SMALL_KIND,))
+        return 0
+
+    lax.fori_loop(0, CTX, first, 0)
+    spread_columns(ls, dcol, doccol)
+
+    def kv_place(late, owner):
+        return pl.ds(pl.multiple_of((owner + late * (2 * CTX - 1 - 2 * owner)) * HALF, HALF), HALF)
+
+    def kv_copy(which, late, owner, place, peer):
+        return pltpu.make_async_remote_copy(
+            src_ref=stage.at[which, kv_place(late, owner), :],
+            dst_ref=terms.at[which, place, pl.ds(pl.multiple_of(late * HALF, HALF), HALF), :],
+            send_sem=kv_send.at[which, late, peer], recv_sem=kv_recv.at[which, late, place],
+            device_id={"ctx": peer}, device_id_type=MESH,
+        )
+
+    def kv_mine(which, late):
+        return pltpu.make_async_copy(
+            stage.at[which, kv_place(late, me), :],
+            terms.at[which, me, pl.ds(pl.multiple_of(late * HALF, HALF), HALF), :],
+            kv_own.at[which, late],
+        )
+
+    def x_copy(owner, place, peer):
+        return pltpu.make_async_remote_copy(
+            src_ref=dx.at[pl.ds(pl.multiple_of(owner * ROWS, ROWS), ROWS), :],
+            dst_ref=grad_x.at[0, :, pl.ds(pl.multiple_of(place * WIDTH, WIDTH), WIDTH)],
+            send_sem=x_send.at[peer], recv_sem=x_recv.at[place],
+            device_id={"ctx": peer}, device_id_type=MESH,
+        )
+
+    def x_mine():
+        return pltpu.make_async_copy(
+            dx.at[pl.ds(pl.multiple_of(me * ROWS, ROWS), ROWS), :],
+            grad_x.at[0, :, pl.ds(pl.multiple_of(me * WIDTH, WIDTH), WIDTH)],
+            x_own,
+        )
+
+    def block(n, _):
         i = SEQ // BLOCK - 1 - n
-        attention_block(i, q, d, k, v, small, dcol, doccol, dk, dv, cot, q2, d2, s_ref, m_ref, l_ref, dq)
+        late = i // 4
+
+        @pl.when(i >= 4)
+        def _():
+            for r in range(4):
+                arrived(28 - 4 * i + r, LATE_KINDS)
+
+        @pl.when(i < 4)
+        def _():
+            for r in range(4):
+                arrived(4 * i + r, EARLY_KINDS)
+
+        attention_block(i, lq, ld, lk, lv, ls, dcol, doccol, dk, dv, cot, q2, d2, s_ref, m_ref, l_ref, dq)
+        rows = pl.ds(pl.multiple_of(i * BLOCK, BLOCK), BLOCK)
+        stage[0, rows, :] = dk[rows, :].astype(BF16)
+        stage[1, rows, :] = dv[rows, :].astype(BF16)
+        for r in range(4):
+            chunk = 4 * i + r
+            owner = chunk + late * (2 * CTX - 1 - 2 * chunk)
+
+            @pl.when(owner != me)
+            def _():
+                for which in range(2):
+                    kv_copy(which, late, owner, me, owner).start()
+
+            @pl.when(owner == me)
+            def _():
+                for which in range(2):
+                    kv_mine(which, late).start()
+
         for sub in (1, 0):
-            ssm_chunk(2 * i + sub, sub * ROWS, x, b, c, small, doccol, cot, skip, spread, gstate, gtimed, acc_a, acc_s, dx)
-        return 0
-
-    lax.fori_loop(0, SEQ // BLOCK, step, 0)
-    gk[...] = dk[...].astype(BF16)
-    gv[...] = dv[...].astype(BF16)
+            owner = 2 * i + sub
+            arrived(owner, SSM_KINDS)
+            ssm_chunk(owner, sub * ROWS, lx, lb, lc, ls, doccol, cot, skip, spread, gstate, gtimed, acc_a, acc_s, dx)
+
+            @pl.when(owner != me)
+            def _():
+                x_copy(owner, me, owner).start()
+
+            @pl.when(owner == me)
+            def _():
+                x_mine().start()
+
+        return 0
+
+    lax.fori_loop(0, SEQ // BLOCK, block, 0)
+
     decay[...] = finish_decay(me, acc_a, acc_s)
 
-
-COMPUTE_SCRATCH = [
+    def ctx_copy(frm, peer):
+        return pltpu.make_async_remote_copy(
+            src_ref=decay, dst_ref=ctx_decay.at[frm], send_sem=ctx_send.at[peer], recv_sem=ctx_recv.at[frm],
+            device_id={"ctx": peer}, device_id_type=MESH,
+        )
+
+    def dp_copy(frm, peer):
+        return pltpu.make_async_remote_copy(
+            src_ref=seq_decay, dst_ref=all_decay.at[frm], send_sem=dp_send.at[peer], recv_sem=dp_recv.at[frm],
+            device_id={"dp": peer}, device_id_type=MESH,
+        )
+
+    def start_ctx(off, _):
+        to = lax.rem(me + off, CTX)
+        ctx_copy(me, to).start()
+        return 0
+
+    lax.fori_loop(1, CTX, start_ctx, 0)
+    ctx_mine = pltpu.make_async_copy(decay, ctx_decay.at[me], ctx_own)
+    ctx_mine.start()
+
+    def end_ctx(off, _):
+        frm = lax.rem(me + CTX - off, CTX)
+        ctx_copy(frm, frm).wait_recv()
+        return 0
+
+    lax.fori_loop(1, CTX, end_ctx, 0)
+    ctx_mine.wait()
+    seq_decay[...] = jnp.sum(ctx_decay[...], axis=0)
+
+    def start_dp(off, _):
+        to = lax.rem(row + off, DP)
+        dp_copy(row, to).start()
+        return 0
+
+    lax.fori_loop(1, DP, start_dp, 0)
+    dp_mine = pltpu.make_async_copy(seq_decay, all_decay.at[row], dp_own)
+    dp_mine.start()
+
+    def end_kv(off, _):
+        frm = lax.rem(me + CTX - off, CTX)
+        for which in range(2):
+            for late in range(2):
+                kv_copy(which, late, me, frm, frm).wait_recv()
+        return 0
+
+    lax.fori_loop(1, CTX, end_kv, 0)
+    for which in range(2):
+        for late in range(2):
+            kv_mine(which, late).wait()
+    for group in range(KVHEADS):
+        cols = pl.ds(group * HEAD_DIM, HEAD_DIM)
+        for which, dst in ((0, grad_k), (1, grad_v)):
+            total = terms[which, 4 * group].astype(F32)
+            for other in range(1, 4):
+                total += terms[which, 4 * group + other].astype(F32)
+            dst[0, :, cols] = total.astype(BF16)
+
+    def end_dp(off, _):
+        frm = lax.rem(row + DP - off, DP)
+        dp_copy(frm, frm).wait_recv()
+        return 0
+
+    lax.fori_loop(1, DP, end_dp, 0)
+    dp_mine.wait()
+    total = all_decay[0]
+    for other in range(1, DP):
+        total += all_decay[other]
+    grad_d[...] = total[:2]
+
+    def end_x(off, _):
+        frm = lax.rem(me + CTX - off, CTX)
+        x_copy(me, frm, frm).wait_recv()
+        return 0
+
+    lax.fori_loop(1, CTX, end_x, 0)
+    x_mine().wait()
+
+    def sent(off, _):
+        to = lax.rem(me + off, CTX)
+        for kind in range(KINDS):
+            in_copy(kind, to, me, to).wait_send()
+        for which in range(2):
+            for late in range(2):
+                kv_copy(which, late, to, me, to).wait_send()
+        x_copy(to, me, to).wait_send()
+        ctx_copy(me, to).wait_send()
+        return 0
+
+    lax.fori_loop(1, CTX, sent, 0)
+
+    def sent_dp(off, _):
+        dp_copy(row, lax.rem(row + off, DP)).wait_send()
+        return 0
+
+    lax.fori_loop(1, DP, sent_dp, 0)
+
+
+DMA = pltpu.SemaphoreType.DMA
+SCRATCH = [
+    pltpu.VMEM((SEQ, WIDTH), BF16),
+    pltpu.VMEM((SEQ, WIDTH), BF16),
+    pltpu.VMEM((SEQ, HEAD_DIM), BF16),
+    pltpu.VMEM((SEQ, HEAD_DIM), BF16),
+    pltpu.VMEM((SEQ, WIDTH), BF16),
+    pltpu.VMEM((SEQ, STATE), BF16),
+    pltpu.VMEM((SEQ, STATE), BF16),
+    pltpu.VMEM((CTX, 24, ROWS), F32),
+    pltpu.VMEM((CTX, 24, ROWS), F32),
+    DMA((KINDS, CTX)),
+    DMA((KINDS, CTX)),
+    DMA((KINDS,)),
     pltpu.VMEM((SEQ, HEAD_DIM), F32),
     pltpu.VMEM((SEQ, HEAD_DIM), F32),
     pltpu.VMEM((BLOCK, WIDTH), BF16),
@@ -399,164 +570,55 @@
     pltpu.VMEM((STATE, WIDTH), F32),
     pltpu.VMEM((ROWS, WIDTH), F32),
     pltpu.VMEM((ROWS, WIDTH), F32),
+    pltpu.VMEM((SEQ, WIDTH), BF16),
+    pltpu.VMEM((2, SEQ, HEAD_DIM), BF16),
+    pltpu.VMEM((2, CTX, ROWS, HEAD_DIM), BF16),
+    DMA((2, 2, CTX)),
+    DMA((2, 2, CTX)),
+    DMA((CTX,)),
+    DMA((CTX,)),
+    DMA((2, 2)),
+    DMA,
+    pltpu.VMEM((8, SSM_HEADS), F32),
+    pltpu.VMEM((CTX, 8, SSM_HEADS), F32),
+    pltpu.VMEM((8, SSM_HEADS), F32),
+    pltpu.VMEM((DP, 8, SSM_HEADS), F32),
+    DMA((CTX,)),
+    DMA((CTX,)),
+    DMA,
+    DMA((DP,)),
+    DMA((DP,)),
+    DMA,
 ]
 
 
-def compute(q, d, k, v, x, b, c, small, skip):
-    vmem = pl.BlockSpec(memory_space=pltpu.VMEM)
-    return pl.pallas_call(
-        compute_kernel,
-        out_shape=[
-            jax.ShapeDtypeStruct((SEQ, WIDTH), BF16),
-            jax.ShapeDtypeStruct((SEQ, HEAD_DIM), BF16),
-            jax.ShapeDtypeStruct((SEQ, HEAD_DIM), BF16),
-            jax.ShapeDtypeStruct((8, SSM_HEADS), F32),
-        ],
-        in_specs=[vmem] * 9,
-        out_specs=[vmem] * 4,
-        scratch_shapes=COMPUTE_SCRATCH,
-        compiler_params=pltpu.CompilerParams(vmem_limit_bytes=48 * 2**20),
-        name="head_gradients",
-    )(q, d, k, v, x, b, c, small, skip)
-
-
-def out_moves(peer, place, arrays, landed):
-    dx, gk, gv, decay = arrays
-    lx, lk, lv, ld = landed
-    early = pl.ds(pl.multiple_of(peer * HALF, HALF), HALF)
-    late = pl.ds(pl.multiple_of((2 * CTX - 1 - peer) * HALF, HALF), HALF)
-    here = pl.ds(pl.multiple_of(peer * ROWS, ROWS), ROWS)
-    wide = pl.ds(pl.multiple_of(place * WIDTH, WIDTH), WIDTH)
-    first, second = pl.ds(0, HALF), pl.ds(HALF, HALF)
-    moves = []
-    for src, dst in ((gk, lk), (gv, lv)):
-        moves.append((src.at[late, :], dst.at[place, second, :]))
-        moves.append((src.at[early, :], dst.at[place, first, :]))
-    moves.append((dx.at[here, :], lx.at[0, :, wide]))
-    moves.append((decay, ld.at[place]))
-    return moves
-
-
-OUT_KINDS = 6
-
-
-def out_kernel(dx, gk, gv, decay, grad_x, grad_k, grad_v, grad_d,
-               lk, lv, ld, seq_decay, all_decay, send_sem, recv_sem, own_sem, dp_send, dp_recv, dp_own):
-    me = lax.axis_index("ctx")
-    row = lax.axis_index("dp")
-    arrays, landed = (dx, gk, gv, decay), (grad_x, lk, lv, ld)
-    greet("ctx", CTX)
-    greet("dp", DP)
-    await_greetings(CTX - 1 + DP - 1)
-
-    def send(off, _):
-        to = lax.rem(me + off, CTX)
-        for kind, (src, dst) in enumerate(out_moves(to, me, arrays, landed)):
-            pltpu.make_async_remote_copy(
-                src_ref=src, dst_ref=dst, send_sem=send_sem.at[kind, to], recv_sem=recv_sem.at[kind, me],
-                device_id={"ctx": to}, device_id_type=MESH,
-            ).start()
-        return 0
-
-    lax.fori_loop(1, CTX, send, 0)
-    own = [pltpu.make_async_copy(src, dst, own_sem.at[kind])
-           for kind, (src, dst) in enumerate(out_moves(me, me, arrays, landed))]
-    for copy in own:
-        copy.start()
-
-    def finish(off, kinds):
-        to = lax.rem(me + off, CTX)
-        frm = lax.rem(me + CTX - off, CTX)
-        gone = out_moves(to, me, arrays, landed)
-        come = out_moves(me, frm, arrays, landed)
-        for kind in kinds:
-            pltpu.make_async_remote_copy(
-                src_ref=gone[kind][0], dst_ref=gone[kind][1], send_sem=send_sem.at[kind, to],
-                recv_sem=recv_sem.at[kind, frm], device_id={"ctx": to}, device_id_type=MESH,
-            ).wait_send()
-            pltpu.make_async_remote_copy(
-                src_ref=come[kind][0], dst_ref=come[kind][1], send_sem=send_sem.at[kind, to],
-                recv_sem=recv_sem.at[kind, frm], device_id={"ctx": to}, device_id_type=MESH,
-            ).wait_recv()
-
-    lax.fori_loop(1, CTX, lambda off, _: (finish(off, (5,)), 0)[1], 0)
-    own[5].wait()
-    seq_decay[...] = jnp.sum(ld[...], axis=0)
-
-    def dp_copy(to, frm):
-        return pltpu.make_async_remote_copy(
-            src_ref=seq_decay, dst_ref=all_decay.at[frm], send_sem=dp_send.at[to], recv_sem=dp_recv.at[frm],
-            device_id={"dp": to}, device_id_type=MESH,
-        )
-
-    lax.fori_loop(1, DP, lambda off, _: (dp_copy(lax.rem(row + off, DP), row).start(), 0)[1], 0)
-    mine = pltpu.make_async_copy(seq_decay, all_decay.at[row], dp_own)
-    mine.start()
-
-    lax.fori_loop(1, CTX, lambda off, _: (finish(off, (0, 1, 2, 3, 4)), 0)[1], 0)
-    for copy in own[:5]:
-        copy.wait()
-    for group in range(KVHEADS):
-        cols = pl.ds(group * HEAD_DIM, HEAD_DIM)
-        for src, dst in ((lk, grad_k), (lv, grad_v)):
-            total = src[4 * group].astype(F32)
-            for other in range(1, 4):
-                total += src[4 * group + other].astype(F32)
-            dst[0, :, cols] = total.astype(BF16)
-
-    def dp_finish(off, _):
-        copy = dp_copy(lax.rem(row + off, DP), lax.rem(row + DP - off, DP))
-        copy.wait_send()
-        copy.wait_recv()
-        return 0
-
-    lax.fori_loop(1, DP, dp_finish, 0)
-    mine.wait()
-    total = all_decay[0]
-    for other in range(1, DP):
-        total += all_decay[other]
-    grad_d[...] = total[:2]
-
-
-def exchange_out(dx, gk, gv, decay):
+def gradients(q, k, v, o, d, ids, x, b, c, step, alog, skip):
     hbm = pl.BlockSpec(memory_space=pl.ANY)
     vmem = pl.BlockSpec(memory_space=pltpu.VMEM)
     return pl.pallas_call(
-        out_kernel,
+        kernel,
         out_shape=[
             jax.ShapeDtypeStruct((1, ROWS, SSM_HEADS * SSM_DIM), BF16),
             jax.ShapeDtypeStruct((1, ROWS, KVHEADS * HEAD_DIM), BF16),
             jax.ShapeDtypeStruct((1, ROWS, KVHEADS * HEAD_DIM), BF16),
             jax.ShapeDtypeStruct((2, SSM_HEADS), F32),
         ],
-        in_specs=[hbm] * 4,
+        in_specs=[hbm] * 7 + [vmem] * 6,
         out_specs=[hbm, vmem, vmem, vmem],
-        scratch_shapes=[
-            pltpu.VMEM((CTX, ROWS, HEAD_DIM), BF16),
-            pltpu.VMEM((CTX, ROWS, HEAD_DIM), BF16),
-            pltpu.VMEM((CTX, 8, SSM_HEADS), F32),
-            pltpu.VMEM((8, SSM_HEADS), F32),
-            pltpu.VMEM((DP, 8, SSM_HEADS), F32),
-            pltpu.SemaphoreType.DMA((OUT_KINDS, CTX)),
-            pltpu.SemaphoreType.DMA((OUT_KINDS, CTX)),
-            pltpu.SemaphoreType.DMA((OUT_KINDS,)),
-            pltpu.SemaphoreType.DMA((DP,)),
-            pltpu.SemaphoreType.DMA((DP,)),
-            pltpu.SemaphoreType.DMA,
-        ],
+        scratch_shapes=SCRATCH,
         compiler_params=pltpu.CompilerParams(
-            collective_id=1, has_side_effects=True, vmem_limit_bytes=32 * 2**20
+            collective_id=0, has_side_effects=True, vmem_limit_bytes=60 * 2**20
         ),
-        name="exchange_out",
-    )(dx, gk, gv, decay)
+        name="gradients",
+    )(q, d, k, v, x, b, c, d, o, ids, step, alog, skip)
 
 
 def shards(queries, keys, values, saved, out_grad, doc_ids, inputs, bmat, cmat, step, alog, skip):
     device = lax.axis_index("ctx")
     own_skip = jnp.repeat(lax.dynamic_slice_in_dim(skip, device * OWN, OWN), SSM_DIM)[None]
-    landed = exchange_in(queries, keys, values, saved, out_grad, doc_ids, inputs, bmat, cmat, step, alog[None])
-    dx, gk, gv, decay = compute(*landed, own_skip)
-    grad_x, grad_k, grad_v, grad_d = exchange_out(dx, gk, gv, decay)
+    grad_x, grad_k, grad_v, grad_d = gradients(
+        queries, keys, values, saved, out_grad, doc_ids, inputs, bmat, cmat, step, alog[None], own_skip
+    )
     return (grad_k, grad_v, grad_x, grad_d)
 
 

time: 213 us -> 133 us (0.62); the launches traced: 210 us -> 133 us
  Pallas kernels: 194 us -> 126 us
  local copies, waits for them, and re-layouts: 15.6 us -> 6.55 us
    pallas_call x3 -> x1, Pallas kernels: 194 us -> 126 us  [gradients(): pl.pallas_call(kernel, out_shape=[jax.ShapeDtypeStruct((1, ROWS, SSM_HEAD...]
    unnamed x32 -> x10, local copies, waits for them, and re-layouts: 15.4 us -> 5.76 us
where the time goes in v2:
time: 133 us
  Pallas kernels  126 us (95%)
  local copies, waits for them, and re-layouts  6.55 us (5%)
    pallas_call x1, Pallas kernels, gradients(): pl.pallas_call(kernel, out_shape=[jax.ShapeDtypeStruct((1, ROWS, SSM_HEAD...  126 us
    unnamed x10, local copies, waits for them, and re-layouts  5.76 us

profile of v2, /device:TPU:1, one launch (start us, length us, event | category | flops | bytes accessed | tf_op | source)
XLA Modules:
  0.0 133.2 jit_solution(1447087306339239273)
XLA Ops:
  0.6 0.0 copy-start.2
  0.6 0.6 copy-done.2
  1.3 0.1 dynamic_slice.3
  1.4 0.1 broadcast_in_dim.7
  1.4 0.6 broadcast_in_dim_reshape.3.skip
  2.1 126.0 %gradients.1 = (bf16[1,128,4096]{2,1,0:T(8,128)(2,1)}, bf16[1,128,512]{2,1,0:T(8,128)(2,1)}, bf16[1,128,512]{2,1,0:T(8,128)(2,1)}, f32[2,128]{1,0:T(2,128)}) custom-call(bf16[1,128,4096]{2,1,0:T(8,128)(2,1)} %q.1, bf16[1,128,4096]{2,1,0:T(8,128)(2,1)} %dvm.1, bf16[1,128,512]{2,1,0:T(8,128)(2,1)} %k.1, bf16[1,128,512]{2,1,0:T(8,128)(2,1)} %v.1, ...), custom_call_target="tpu_custom_call" | custom-call | tf_op jit(solution)/shard_map/gradients/pallas_call | solution.py:598
  128.1 0.0 copy-start
  128.1 1.6 %copy.20 = bf16[1,128,512]{2,1,0:T(8,128)(2,1)} copy(bf16[1,128,512]{2,1,0:T(8,128)(2,1)} %get-tuple-element.16) | data formatting | bytes 262144
  129.7 0.0 copy-done
  129.7 0.7 copy.21
  130.3 0.0 copy-start.1
  130.3 2.3 %copy.22 = bf16[1,128,4096]{2,1,0:T(8,128)(2,1)} copy(bf16[1,128,4096]{2,1,0:T(8,128)(2,1)} %get-tuple-element.18) | data formatting | bytes 2097152
  132.6 0.0 copy-done.1
  132.6 0.6 copy.23
Async XLA Ops:
  0.6 0.7 copy-start.2
  128.1 1.6 %copy-start = (bf16[1,128,512]{2,1,0:T(8,128)(2,1)S(1)}, bf16[1,128,512]{2,1,0:T(8,128)(2,1)}, u32[]{:S(2)}) copy-start(bf16[1,128,512]{2,1,0:T(8,128)(2,1)} %get-tuple-element.17) | copy-start | bytes 393220
  130.3 2.3 %copy-start.1 = (f32[2,128]{1,0:T(2,128)S(1)}, f32[2,128]{1,0:T(2,128)}, u32[]{:S(2)}) copy-start(f32[2,128]{1,0:T(2,128)} %get-tuple-element.19) | copy-start | bytes 3076

commit v3 on v2

v3 whole, which is shorter than its diff:
```python
import jax
import jax.numpy as jnp
from jax import lax
from jax.experimental import pallas as pl
from jax.experimental.pallas import tpu as pltpu
from jax.sharding import PartitionSpec as P

QHEADS = 32
KVHEADS = 4
HEAD_DIM = 128
SSM_HEADS = 128
SSM_DIM = 32
STATE = 128
SEQ = 2048
ROWS = 128
HALF = 64
CTX = 16
DP = 8
WIDTH = 256
OWN = 8
QCOLS = 512
BLOCK = 256
SPAN = 5
SCALE = HEAD_DIM ** (-0.5)
FAR = -1e30

MESH = pl.DeviceIdType.MESH
HIGHEST = lax.Precision.HIGHEST
F32 = jnp.float32
BF16 = jnp.bfloat16


def dot(a, b, dims, precision=None):
    return lax.dot_general(a, b, (dims, ((), ())), precision=precision, preferred_element_type=F32)


NN = ((1,), (0,))
NT = ((1,), (1,))
TN = ((0,), (0,))


def three(a):
    high = a.astype(BF16)
    rest = a - high.astype(F32)
    mid = rest.astype(BF16)
    low = (rest - mid.astype(F32)).astype(BF16)
    return high, mid, low


def greet(axis, count):
    me = lax.axis_index(axis)
    barrier = pltpu.get_barrier_semaphore()

    def one(off, _):
        pl.semaphore_signal(barrier, inc=1, device_id={axis: lax.rem(me + off, count)}, device_id_type=MESH)
        return 0

    lax.fori_loop(1, count, one, 0)


def await_greetings(total):
    pl.semaphore_wait(pltpu.get_barrier_semaphore(), total)


def slot(device):
    return device // 4 * 4 + device % 2 * 2 + device // 2 % 2


def early_rows(device):
    return pl.ds(pl.multiple_of(device * HALF, HALF), HALF)


def late_rows(device):
    return pl.ds(pl.multiple_of((2 * CTX - 1 - device) * HALF, HALF), HALF)


def device_rows(device):
    return pl.ds(pl.multiple_of(device * ROWS, ROWS), ROWS)


def block_rows(i):
    return pl.ds(pl.multiple_of(i * BLOCK, BLOCK), BLOCK)


def columns(start, width):
    return pl.ds(pl.multiple_of(start * width, width), width)


def pack_small(out_grad, saved, ids, step, alog, small):
    ones = jnp.ones((8, HEAD_DIM), F32)
    sub = lax.broadcasted_iota(jnp.int32, (8, ROWS), 0)
    docs = jnp.broadcast_to(ids[...].astype(F32), (8, ROWS))
    rate = step[0] * -jnp.exp(alog[...])
    upto = lax.broadcasted_iota(jnp.int32, (ROWS, ROWS), 0) <= lax.broadcasted_iota(jnp.int32, (ROWS, ROWS), 1)
    totals = dot(rate, upto.astype(F32), TN, HIGHEST)
    steps = step[0].T
    for j in range(CTX):
        at = 8 * slot(j)
        small[j, 0:8, :] = steps[at : at + 8]
        small[j, 8:16, :] = totals[at : at + 8]

    def one(pair, _):
        tile = docs
        for e in range(4):
            cols = columns(4 * pair + e, HEAD_DIM)
            product = out_grad[0, :, cols].astype(F32) * saved[0, :, cols].astype(F32)
            tile = jnp.where(sub == e, dot(ones, product, NT, HIGHEST), tile)
        for z in range(2):
            small[pair // 2 * 4 + 2 * z + pair % 2, 16:24, :] = tile
        return 0

    lax.fori_loop(0, CTX // 2, one, 0)


def spread_columns(small, zz, dcol, doccol):
    row = lax.broadcasted_iota(jnp.int32, (24, 5 * ROWS), 0) % 8
    lane = lax.broadcasted_iota(jnp.int32, (24, 5 * ROWS), 1) // ROWS
    pick = jnp.where(row == lane, 1.0, 0.0).astype(BF16)
    doccol[0:8, :] = jnp.full((8, ROWS), -1.0, F32)

    def one(src, _):
        parts = jnp.concatenate([p.astype(F32) for p in three(small[src, 16:24, :])], axis=0).astype(BF16)
        wide = dot(parts, pick, TN)
        doccol[pl.ds(pl.multiple_of(8 + src * ROWS, 8), ROWS), :] = wide[:, 4 * ROWS :]

        @pl.when(src // 2 % 2 == zz)
        def _():
            dcol[query_rows(src, 0), :] = wide[:HALF, : 4 * ROWS]
            dcol[query_rows(src, 1), :] = wide[HALF:, : 4 * ROWS]

        return 0

    lax.fori_loop(0, CTX, one, 0)


def query_rows(src, late):
    block = src // 4 + late * (7 - 2 * (src // 4))
    second = src % 2 + late * (1 - 2 * (src % 2))
    return pl.ds(pl.multiple_of(block * ROWS + second * HALF, HALF), HALF)


def attention_block(i, off, q, d, kv, small, dcol, doccol, dkv, q2, d2, s_ref, m_ref, l_ref, dq):
    rows = device_rows(i)
    for h in range(4):
        part = pl.ds(h * ROWS, ROWS)
        q2[part, :] = q[rows, h * HEAD_DIM : (h + 1) * HEAD_DIM]
        d2[part, :] = d[rows, h * HEAD_DIM : (h + 1) * HEAD_DIM]
    m_ref[...] = jnp.full(m_ref.shape, FAR, F32)
    l_ref[...] = jnp.zeros(l_ref.shape, F32)
    dq[...] = jnp.zeros(dq.shape, F32)
    first = jnp.maximum(i - (SPAN - 1), 0)
    ahead = lax.broadcasted_iota(jnp.int32, (ROWS, BLOCK), 0) - lax.broadcasted_iota(jnp.int32, (ROWS, BLOCK), 1)

    def scores(j, _):
        keys = kv[0, block_rows(j), :]
        own = doccol[pl.ds(pl.multiple_of(8 + i * BLOCK + off, 8), ROWS), :]
        own = jnp.concatenate([own, own], axis=1)
        theirs = jnp.concatenate([small[2 * j, 20:21, :], small[2 * j + 1, 20:21, :]], axis=1)
        allowed = (own == theirs) & (ahead >= (j - i) * BLOCK - off)
        for h in range(4):
            part = pl.ds(h * ROWS, ROWS)
            s = jnp.where(allowed, dot(q2[part, :], keys, NT), FAR)
            s_ref[j - first, part, :] = s
            m_ref[part, :] = jnp.maximum(m_ref[part, :], jnp.maximum(s[:, :ROWS], s[:, ROWS:]))
        return 0

    lax.fori_loop(first, i + 1, scores, 0)
    m_ref[...] = jnp.broadcast_to(jnp.max(m_ref[...], axis=1, keepdims=True), m_ref.shape)

    def exps(j, _):
        for h in range(4):
            part = pl.ds(h * ROWS, ROWS)
            m = m_ref[part, :]
            e = jnp.exp((s_ref[j - first, part, :] - jnp.concatenate([m, m], axis=1)) * SCALE)
            s_ref[j - first, part, :] = e
            l_ref[part, :] += e[:, :ROWS] + e[:, ROWS:]
        return 0

    lax.fori_loop(first, i + 1, exps, 0)
    l_ref[...] = jnp.broadcast_to(1.0 / jnp.sum(l_ref[...], axis=1, keepdims=True), l_ref.shape)

    def grads(j, _):
        there = block_rows(j)
        keys, vals = kv[0, there, :], kv[1, there, :]
        probs, scaled = [], []
        for h in range(4):
            part = pl.ds(h * ROWS, ROWS)
            inv = l_ref[part, :]
            p = s_ref[j - first, part, :] * jnp.concatenate([inv, inv], axis=1)
            delta = dcol[rows, h * ROWS : (h + 1) * ROWS]
            dp = dot(d2[part, :], vals, NT) - jnp.concatenate([delta, delta], axis=1)
            ds = (p * dp * SCALE).astype(BF16)
            dq[part, :] += dot(ds, keys, NN)
            probs.append(p.astype(BF16))
            scaled.append(ds)
        dkv[0, there, :] += dot(jnp.concatenate(scaled, axis=0), q2[...], TN)
        dkv[1, there, :] += dot(jnp.concatenate(probs, axis=0), d2[...], TN)
        return 0

    lax.fori_loop(first, i + 1, grads, 0)


def spread_matrix(spread):
    row = lax.broadcasted_iota(jnp.int32, spread.shape, 0)
    lane = lax.broadcasted_iota(jnp.int32, spread.shape, 1)
    head = row % OWN
    a = (lane < 1024) & (row < 24) & (lane // ROWS == head)
    b = (lane >= 1024) & (lane < 1280) & (row < 24) & ((lane - 1024) // SSM_DIM == head)
    c = (lane >= 1280) & (row >= 24) & ((lane - 1280) // SSM_DIM == head)
    spread[...] = jnp.where(a | b | c, 1.0, 0.0).astype(BF16)


def ssm_chunk(c, x, bcm, small, doccol, cot, skip, spread, gstate, gtimed, acc_a, acc_s, dx):
    base = pl.multiple_of(c * ROWS, ROWS)
    here = pl.ds(base, ROWS)
    bc, cc = bcm[0, here, :], bcm[1, here, :]
    xc = x[here, :].astype(F32)
    dyb = cot[here, :]
    dy = dyb.astype(F32)
    steps, totals = small[c, 0:8, :], small[c, 8:16, :]
    parts = jnp.concatenate([p.astype(F32) for p in three(totals) + three(steps)], axis=0).astype(BF16)
    wide = dot(parts, spread[...], TN)
    te, se = wide[:, 1024:1280], wide[:, 1280:1536]
    docs = doccol[pl.ds(pl.multiple_of(8 + base, 8), ROWS), :]
    before = doccol[pl.ds(7 + base, 1), :]
    last = doccol[pl.ds(7 + ROWS + base, 1), :]
    docrow = small[c, 20:21, :]
    sub = lax.broadcasted_iota(jnp.int32, (ROWS, ROWS), 0)
    lane = lax.broadcasted_iota(jnp.int32, (ROWS, ROWS), 1)
    inner = jnp.where((sub <= lane) & (docs == docrow), dot(bc, cc, NT), 0.0)

    plain, timed = [], []
    for half in range(2):
        dyh = dyb[:, half * 128 : half * 128 + 128]
        total = None
        for pair in range(2):
            tops, lows, rights = [], [], []
            for one in range(2):
                local = 2 * pair + one
                h = 4 * half + local
                gap = totals[h : h + 1, :] - wide[:, ROWS * h : ROWS * h + ROWS]
                w = inner * jnp.exp(gap)
                tops.append(w.astype(BF16))
                lows.append((w * gap).astype(BF16))
                rights.append(jnp.where(lane // SSM_DIM == local, dyh.astype(F32), 0.0).astype(BF16))
            left = jnp.concatenate([jnp.concatenate(tops, axis=1), jnp.concatenate(lows, axis=1)], axis=0)
            out = dot(left, jnp.concatenate(rights, axis=0), NN)
            total = out if total is None else total + out
        plain.append(total[:ROWS])
        timed.append(total[ROWS:])
    intra = jnp.concatenate(plain, axis=1)
    intra_t = jnp.concatenate(timed, axis=1)

    both = jnp.concatenate([gstate[...], gtimed[...]], axis=1).astype(BF16)
    inter = dot(bc, both, NN)
    te_last = te[ROWS - 1 : ROWS, :]
    docs2 = jnp.concatenate([docs, docs], axis=1)
    before2 = jnp.concatenate([before, before], axis=1)
    last2 = jnp.concatenate([last, last], axis=1)
    left_time = te_last - te
    leave = jnp.where(docs2 == last2, jnp.exp(left_time), 0.0)
    got = intra + leave * inter[:, :WIDTH]
    got_t = intra_t + leave * (left_time * inter[:, :WIDTH] + inter[:, WIDTH:])
    dx[here, :] = (se * got + skip[0:1, :] * dy).astype(BF16)
    acc_a[...] += se * xc * got_t
    acc_s[...] += dy * xc

    enter = jnp.where(docs2 == before2, jnp.exp(te), 0.0)
    dye = dy * enter
    fresh = dot(cc, jnp.concatenate([dye, dye * te], axis=1).astype(BF16), TN)
    whole = jnp.where(last2 == before2, jnp.exp(te_last), 0.0)
    old = gstate[...]
    gtimed[...] = whole * (gtimed[...] + te_last * old) + fresh[:, WIDTH:]
    gstate[...] = whole * old + fresh[:, :WIDTH]


def own_heads(me):
    row = lax.broadcasted_iota(jnp.int32, (SSM_HEADS, WIDTH), 0)
    lane = lax.broadcasted_iota(jnp.int32, (SSM_HEADS, WIDTH), 1)
    return jnp.where(lane // SSM_DIM + slot(me) * OWN == row, 1.0, 0.0)


def finish_decay(me, acc_a, acc_s):
    sums = jnp.concatenate(
        [jnp.sum(acc_a[...], axis=0, keepdims=True), jnp.sum(acc_s[...], axis=0, keepdims=True), jnp.zeros((6, WIDTH), F32)],
        axis=0,
    )
    return dot(sums, own_heads(me), NT, HIGHEST)


BLOCKS = SEQ // BLOCK
KV_EARLY, KV_LATE, BC = range(3)


def kernel(q, d, k, v, x, b, c, dvm, o, ids, step, alog, skip_in,
           grad_x, grad_kv, grad_d,
           lq, ld, lkv, lbc, lx, ls, small,
           x_in_send, x_in_recv, small_send, small_recv, first_send, first_recv,
           z_send, core_send, relay_send, fwd_recv, q_send, q_recv, own_sem,
           dkv, q2, d2, s_ref, m_ref, l_ref, dq, dcol, doccol, spread, gstate, gtimed, acc_a, acc_s, skip,
           dx, x_send, x_recv, x_own,
           cot, cot_out, cot_send, cot_recv,
           pair_in, pair_send, pair_recv, half_out, half_in, half_send, half_recv,
           done, done_send, done_recv, done_own,
           decay, ctx_decay, seq_decay, all_decay, ctx_send, ctx_recv, ctx_own, dp_send, dp_recv, dp_own):
    me = lax.axis_index("ctx")
    row = lax.axis_index("dp")
    xx, zz, cc, zc = me // 4, me // 2 % 2, me % 2, me % 4
    core_peer = me + 1 - 2 * cc
    z_peer = me + 2 - 4 * zz
    first, second = pl.ds(0, HALF), pl.ds(HALF, HALF)

    def remote(src, dst, send_sem, recv_sem, peer):
        return pltpu.make_async_remote_copy(
            src_ref=src, dst_ref=dst, send_sem=send_sem, recv_sem=recv_sem,
            device_id={"ctx": peer}, device_id_type=MESH,
        )

    def group_moves(plane, frm):
        cols = columns(plane, HEAD_DIM)
        return [
            (k.at[0, first, cols], lkv.at[0, early_rows(frm), :]),
            (v.at[0, first, cols], lkv.at[1, early_rows(frm), :]),
            (k.at[0, second, cols], lkv.at[0, late_rows(frm), :]),
            (v.at[0, second, cols], lkv.at[1, late_rows(frm), :]),
            (b.at[0, :, cols], lbc.at[0, device_rows(frm), :]),
            (c.at[0, :, cols], lbc.at[1, device_rows(frm), :]),
        ]

    def first_copy(kind, to, frm, peer):
        src, dst = group_moves(to // 4, frm)[kind]
        return remote(src, dst, first_send.at[kind, peer // 4], first_recv.at[kind, frm], peer)

    def landed(kind, src):
        return (
            lkv.at[:, early_rows(src), :],
            lkv.at[:, late_rows(src), :],
            lbc.at[:, device_rows(src), :],
        )[kind]

    def forward(kind, src, sems, peer):
        ref = landed(kind, src)
        return remote(ref, ref, sems.at[kind, src // 4], fwd_recv.at[kind, src], peer)

    def others_x(body):
        def one(n, _):
            body(lax.rem(xx + n, 4) * 4 + zc)
            return 0

        lax.fori_loop(1, 4, one, 0)

    def each_x(body):
        def one(n, _):
            body(lax.rem(xx + n, 4) * 4 + zc)
            return 0

        lax.fori_loop(0, 4, one, 0)

    def send_first(kinds):
        others_x(lambda to: [first_copy(kind, to, me, to).start() for kind in kinds])

    def q_copy(array, late, to, frm, peer):
        src = ((q, d)[array]).at[0, pl.ds(late * HALF, HALF), columns(to // 4 * 2 + to % 2, QCOLS)]
        dst = ((lq, ld)[array]).at[query_rows(frm, late), :]
        return remote(src, dst, q_send.at[2 * array + late, peer], q_recv.at[2 * array + late, frm], peer)

    def send_q(late):
        def one(n, _):
            to = lax.rem(xx + n // 2, 4) * 4 + 2 * zz + lax.rem(cc + n, 2)
            for array in range(2):
                q_copy(array, late, to, me, to).start()
            return 0

        lax.fori_loop(1, 8, one, 0)

    def q_arrived(src, late):
        @pl.when(src != me)
        def _():
            for array in range(2):
                q_copy(array, late, me, src, src).wait_recv()

    def x_in_copy(to, frm, peer):
        return remote(x.at[0, :, columns(slot(to), WIDTH)], lx.at[device_rows(frm), :],
                      x_in_send.at[peer], x_in_recv.at[frm], peer)

    def small_copy(to, frm, peer):
        return remote(small.at[to], ls.at[frm], small_send.at[peer], small_recv.at[frm], peer)

    def to_all(body):
        def one(n, _):
            body(lax.rem(me + n, CTX))
            return 0

        lax.fori_loop(1, CTX, one, 0)

    def own_copies():
        moves = group_moves(xx, me)
        for array in range(2):
            for late in range(2):
                moves.append((((q, d)[array]).at[0, pl.ds(late * HALF, HALF), columns(xx * 2 + cc, QCOLS)],
                              ((lq, ld)[array]).at[query_rows(me, late), :]))
        moves.append((x.at[0, :, columns(slot(me), WIDTH)], lx.at[device_rows(me), :]))
        moves.append((small.at[me], ls.at[me]))
        return [pltpu.make_async_copy(src, dst, own_sem.at[n]) for n, (src, dst) in enumerate(moves)]

    greet("ctx", CTX)
    greet("dp", DP)
    await_greetings(CTX - 1 + DP - 1)
    send_first((0, 1, 2, 3))
    own = own_copies()
    for copy in own[:-1]:
        copy.start()
    send_q(1)
    send_first((4, 5))
    pack_small(dvm, o, ids, step, alog, small)
    to_all(lambda to: small_copy(to, me, to).start())
    own[-1].start()
    for copy in own:
        copy.wait()

    def pass_on(kinds, parts):
        def one(src):
            @pl.when(src != me)
            def _():
                for kind in kinds:
                    first_copy(kind, me, src, src).wait_recv()

            for part in parts:
                forward(part, src, z_send, z_peer).start()
                forward(part, src, core_send, core_peer).start()

        each_x(one)

    def relay(parts):
        def one(src):
            src = src + 2 - 4 * zz
            for part in parts:
                forward(part, src, z_send, z_peer).wait_recv()
                forward(part, src, relay_send, core_peer).start()

        each_x(one)

    pass_on((0, 1, 2, 3), (KV_EARLY, KV_LATE))

    @pl.when(me >= CTX // 2)
    def _():
        to_all(lambda to: x_in_copy(to, me, to).start())

    send_q(0)

    @pl.when(me < CTX // 2)
    def _():
        to_all(lambda to: x_in_copy(to, me, to).start())

    pass_on((4, 5), (BC,))
    relay((KV_EARLY, KV_LATE))

    for ref in (dkv, gstate, gtimed, acc_a, acc_s):
        ref[...] = jnp.zeros(ref.shape, F32)
    skip[...] = dot(jnp.broadcast_to(skip_in[...], (8, SSM_HEADS)), own_heads(me), NN, HIGHEST)
    spread_matrix(spread)

    to_all(lambda src: small_copy(me, src, src).wait_recv())
    spread_columns(ls, zz, dcol, doccol)

    def from_core(parts):
        def one(src):
            for flip in (0, 1):
                at = src + 1 - 2 * cc + flip * (2 - 4 * zz)
                for part in parts:
                    forward(part, at, core_send, core_peer).wait_recv()

        each_x(one)

    from_core((KV_EARLY, KV_LATE))
    relay((BC,))

    def x_copy(to, frm, peer):
        return remote(dx.at[device_rows(to), :], grad_x.at[0, :, columns(slot(frm), WIDTH)],
                      x_send.at[peer], x_recv.at[frm], peer)

    def x_mine():
        return pltpu.make_async_copy(dx.at[device_rows(me), :], grad_x.at[0, :, columns(slot(me), WIDTH)], x_own)

    def own_off(i):
        late = i // 4
        return (zz + late - 2 * zz * late) * ROWS

    def cot_copy(i, off):
        return remote(cot_out.at[i], cot.at[pl.ds(pl.multiple_of(i * BLOCK + off, ROWS), ROWS), :],
                      cot_send.at[i], cot_recv.at[i], z_peer)

    def pair_copy(i, which):
        return remote(dkv.at[which, block_rows(i), :], pair_in.at[i], pair_send.at[i], pair_recv.at[i], core_peer)

    def half_copy(i):
        return remote(half_out.at[i], half_in.at[i], half_send.at[i], half_recv.at[i], z_peer)

    def done_owner(i, r):
        late = i // 4
        chunk = 4 * i + own_off(i) // HALF + r
        return chunk + late * (2 * CTX - 1 - 2 * chunk)

    def done_copy(i, r, core, plane, late, peer):
        return remote(done.at[i, pl.ds(r * HALF, HALF), :],
                      grad_kv.at[core, pl.ds(pl.multiple_of(late * HALF, HALF), HALF), columns(plane, HEAD_DIM)],
                      done_send.at[i, r], done_recv.at[core, late, plane], peer)

    def done_mine(i, r):
        late = i // 4
        return pltpu.make_async_copy(
            done.at[i, pl.ds(r * HALF, HALF), :],
            grad_kv.at[cc, pl.ds(pl.multiple_of(late * HALF, HALF), HALF), columns(xx, HEAD_DIM)],
            done_own.at[late],
        )

    def sum_pair(i):
        pair_copy(i, 1 - cc).wait_recv()
        off = ROWS - own_off(i)
        there = pl.ds(pl.multiple_of(i * BLOCK + off, ROWS), ROWS)
        half_out[i] = (dkv[cc, there, :] + pair_in[i, pl.ds(pl.multiple_of(off, ROWS), ROWS), :]).astype(BF16)
        half_copy(i).start()

    def sum_half(i):
        half_copy(i).wait_recv()
        off = own_off(i)
        there = pl.ds(pl.multiple_of(i * BLOCK + off, ROWS), ROWS)
        mine = dkv[cc, there, :] + pair_in[i, pl.ds(pl.multiple_of(off, ROWS), ROWS), :]
        done[i] = (mine + half_in[i].astype(F32)).astype(BF16)
        for r in range(2):
            owner = done_owner(i, r)

            @pl.when(owner != me)
            def _():
                done_copy(i, r, cc, xx, i // 4, owner).start()

            @pl.when(owner == me)
            def _():
                done_mine(i, r).start()

    def block(n, _):
        @pl.when(n < BLOCKS)
        def _():
            i = BLOCKS - 1 - n
            off = own_off(i)

            @pl.when(i >= 4)
            def _():
                for r in range(2):
                    q_arrived(4 * (7 - i) + 2 * zz + r, 1)

            @pl.when(i < 4)
            def _():
                for r in range(2):
                    q_arrived(4 * i + 2 * zz + r, 0)

            attention_block(i, off, lq, ld, lkv, ls, dcol, doccol, dkv, q2, d2, s_ref, m_ref, l_ref, dq)
            pair_copy(i, 1 - cc).start()
            here = pl.ds(pl.multiple_of(i * BLOCK + off, ROWS), ROWS)
            for e in range(2):
                cols = slice(e * HEAD_DIM, (e + 1) * HEAD_DIM)
                mine = pl.ds(pl.multiple_of((2 * zz + e) * ROWS, ROWS), ROWS)
                theirs = pl.ds(pl.multiple_of((2 - 2 * zz + e) * ROWS, ROWS), ROWS)
                cot[here, cols] = dq[mine, :].astype(BF16)
                cot_out[i, :, cols] = dq[theirs, :].astype(BF16)
            cot_copy(i, off).start()

        @pl.when(n == 0)
        def _():
            from_core((BC,))

        @pl.when(n >= 1)
        def _():
            sum_pair(BLOCKS - n)

        @pl.when(n >= 2)
        def _():
            sum_half(BLOCKS + 1 - n)

        @pl.when(n >= 1)
        def _():
            i = BLOCKS - n
            cot_copy(i, ROWS - own_off(i)).wait_recv()
            for sub in (1, 0):
                owner = 2 * i + sub

                @pl.when(owner != me)
                def _():
                    x_in_copy(me, owner, owner).wait_recv()

                ssm_chunk(owner, lx, lbc, ls, doccol, cot, skip, spread, gstate, gtimed, acc_a, acc_s, dx)

                @pl.when(owner != me)
                def _():
                    x_copy(owner, me, owner).start()

                @pl.when(owner == me)
                def _():
                    x_mine().start()

        return 0

    lax.fori_loop(0, BLOCKS + 1, block, 0)

    decay[...] = finish_decay(me, acc_a, acc_s)

    def ctx_copy(frm, peer):
        return remote(decay, ctx_decay.at[frm], ctx_send.at[peer], ctx_recv.at[frm], peer)

    def dp_copy(frm, peer):
        return pltpu.make_async_remote_copy(
            src_ref=seq_decay, dst_ref=all_decay.at[frm], send_sem=dp_send.at[peer], recv_sem=dp_recv.at[frm],
            device_id={"dp": peer}, device_id_type=MESH,
        )

    to_all(lambda to: ctx_copy(me, to).start())
    ctx_mine = pltpu.make_async_copy(decay, ctx_decay.at[me], ctx_own)
    ctx_mine.start()
    sum_half(0)
    to_all(lambda frm: ctx_copy(frm, frm).wait_recv())
    ctx_mine.wait()
    seq_decay[...] = jnp.sum(ctx_decay[...], axis=0)

    def start_dp(off, _):
        dp_copy(row, lax.rem(row + off, DP)).start()
        return 0

    lax.fori_loop(1, DP, start_dp, 0)
    dp_mine = pltpu.make_async_copy(seq_decay, all_decay.at[row], dp_own)
    dp_mine.start()

    def sent(to):
        small_copy(to, me, to).wait_send()
        x_in_copy(to, me, to).wait_send()
        x_copy(to, me, to).wait_send()
        ctx_copy(me, to).wait_send()

    to_all(sent)
    others_x(lambda to: [first_copy(kind, to, me, to).wait_send() for kind in range(6)])

    def forwarded(src):
        other = src + 2 - 4 * zz
        for part in range(3):
            forward(part, src, z_send, z_peer).wait_send()
            forward(part, src, core_send, core_peer).wait_send()
            forward(part, other, relay_send, core_peer).wait_send()

    each_x(forwarded)

    def sent_q(n, _):
        to = lax.rem(xx + n // 2, 4) * 4 + 2 * zz + lax.rem(cc + n, 2)
        for array in range(2):
            for late in range(2):
                q_copy(array, late, to, me, to).wait_send()
        return 0

    lax.fori_loop(1, 8, sent_q, 0)

    def sent_blocks(i, _):
        cot_copy(i, own_off(i)).wait_send()
        pair_copy(i, 1 - cc).wait_send()
        half_copy(i).wait_send()
        for r in range(2):
            owner = done_owner(i, r)

            @pl.when(owner != me)
            def _():
                done_copy(i, r, cc, xx, i // 4, owner).wait_send()

            @pl.when(owner == me)
            def _():
                done_mine(i, r).wait()

        return 0

    lax.fori_loop(0, BLOCKS, sent_blocks, 0)

    for core in range(2):
        for late in range(2):
            for plane in range(4):
                @pl.when(plane * 4 + 2 * zz + core != me)
                def _():
                    done_copy(0, 0, core, plane, late, core_peer).wait_recv()

    def end_dp(off, _):
        frm = lax.rem(row + DP - off, DP)
        dp_copy(frm, frm).wait_recv()
        dp_copy(row, frm).wait_send()
        return 0

    lax.fori_loop(1, DP, end_dp, 0)
    dp_mine.wait()
    total = all_decay[0]
    for other in range(1, DP):
        total += all_decay[other]
    grad_d[...] = total[:2]
    to_all(lambda frm: x_copy(me, frm, frm).wait_recv())
    x_mine().wait()


DMA = pltpu.SemaphoreType.DMA
SCRATCH = [
    pltpu.VMEM((SEQ // 2, QCOLS), BF16),
    pltpu.VMEM((SEQ // 2, QCOLS), BF16),
    pltpu.VMEM((2, SEQ, HEAD_DIM), BF16),
    pltpu.VMEM((2, SEQ, STATE), BF16),
    pltpu.VMEM((SEQ, WIDTH), BF16),
    pltpu.VMEM((CTX, 24, ROWS), F32),
    pltpu.VMEM((CTX, 24, ROWS), F32),
    DMA((CTX,)),
    DMA((CTX,)),
    DMA((CTX,)),
    DMA((CTX,)),
    DMA((6, 4)),
    DMA((6, CTX)),
    DMA((3, 4)),
    DMA((3, 4)),
    DMA((3, 4)),
    DMA((3, CTX)),
    DMA((4, CTX)),
    DMA((4, CTX)),
    DMA((12,)),
    pltpu.VMEM((2, SEQ, HEAD_DIM), F32),
    pltpu.VMEM((4 * ROWS, HEAD_DIM), BF16),
    pltpu.VMEM((4 * ROWS, HEAD_DIM), BF16),
    pltpu.VMEM((SPAN, 4 * ROWS, BLOCK), F32),
    pltpu.VMEM((4 * ROWS, ROWS), F32),
    pltpu.VMEM((4 * ROWS, ROWS), F32),
    pltpu.VMEM((4 * ROWS, HEAD_DIM), F32),
    pltpu.VMEM((SEQ // 2, 4 * ROWS), F32),
    pltpu.VMEM((SEQ + 8, ROWS), F32),
    pltpu.VMEM((48, 1536), BF16),
    pltpu.VMEM((STATE, WIDTH), F32),
    pltpu.VMEM((STATE, WIDTH), F32),
    pltpu.VMEM((ROWS, WIDTH), F32),
    pltpu.VMEM((ROWS, WIDTH), F32),
    pltpu.VMEM((8, WIDTH), F32),
    pltpu.VMEM((SEQ, WIDTH), BF16),
    DMA((CTX,)),
    DMA((CTX,)),
    DMA,
    pltpu.VMEM((SEQ, WIDTH), BF16),
    pltpu.VMEM((BLOCKS, ROWS, WIDTH), BF16),
    DMA((BLOCKS,)),
    DMA((BLOCKS,)),
    pltpu.VMEM((BLOCKS, BLOCK, HEAD_DIM), F32),
    DMA((BLOCKS,)),
    DMA((BLOCKS,)),
    pltpu.VMEM((BLOCKS, ROWS, HEAD_DIM), BF16),
    pltpu.VMEM((BLOCKS, ROWS, HEAD_DIM), BF16),
    DMA((BLOCKS,)),
    DMA((BLOCKS,)),
    pltpu.VMEM((BLOCKS, ROWS, HEAD_DIM), BF16),
    DMA((BLOCKS, 2)),
    DMA((2, 2, 4)),
    DMA((2,)),
    pltpu.VMEM((8, SSM_HEADS), F32),
    pltpu.VMEM((CTX, 8, SSM_HEADS), F32),
    pltpu.VMEM((8, SSM_HEADS), F32),
    pltpu.VMEM((DP, 8, SSM_HEADS), F32),
    DMA((CTX,)),
    DMA((CTX,)),
    DMA,
    DMA((DP,)),
    DMA((DP,)),
    DMA,
]


def gradients(q, k, v, o, d, ids, x, b, c, step, alog, skip):
    hbm = pl.BlockSpec(memory_space=pl.ANY)
    vmem = pl.BlockSpec(memory_space=pltpu.VMEM)
    return pl.pallas_call(
        kernel,
        out_shape=[
            jax.ShapeDtypeStruct((1, ROWS, SSM_HEADS * SSM_DIM), BF16),
            jax.ShapeDtypeStruct((2, ROWS, KVHEADS * HEAD_DIM), BF16),
            jax.ShapeDtypeStruct((2, SSM_HEADS), F32),
        ],
        in_specs=[hbm] * 7 + [vmem] * 6,
        out_specs=[hbm, hbm, vmem],
        scratch_shapes=SCRATCH,
        compiler_params=pltpu.CompilerParams(
            collective_id=0, has_side_effects=True, vmem_limit_bytes=60 * 2**20
        ),
        name="gradients",
    )(q, d, k, v, x, b, c, d, o, ids, step, alog, skip)


def settle_kernel(x, kv, dec, grad_k, grad_v, grad_x, grad_d):
    grad_x[...] = x[...]
    grad_k[0] = kv[0]
    grad_v[0] = kv[1]
    grad_d[...] = dec[...]


def settle(x, kv, dec):
    vmem = pl.BlockSpec(memory_space=pltpu.VMEM)
    narrow = jax.ShapeDtypeStruct((1, ROWS, KVHEADS * HEAD_DIM), BF16)
    return pl.pallas_call(
        settle_kernel,
        out_shape=[narrow, narrow, jax.ShapeDtypeStruct(x.shape, BF16), jax.ShapeDtypeStruct(dec.shape, F32)],
        in_specs=[vmem] * 3,
        out_specs=[vmem] * 4,
        compiler_params=pltpu.CompilerParams(vmem_limit_bytes=60 * 2**20),
        name="settle",
    )(x, kv, dec)


def shards(queries, keys, values, saved, out_grad, doc_ids, inputs, bmat, cmat, step, alog, skip):
    return tuple(settle(*gradients(
        queries, keys, values, saved, out_grad, doc_ids, inputs, bmat, cmat, step, alog[None], skip[None]
    )))


def solution(mesh):
    return jax.shard_map(
        shards,
        mesh=mesh,
        in_specs=(
            P("dp", "ctx", None),
            P("dp", "ctx", None),
            P("dp", "ctx", None),
            P("dp", "ctx", None),
            P("dp", "ctx", None),
            P("dp", "ctx"),
            P("dp", "ctx", None),
            P("dp", "ctx", None),
            P("dp", "ctx", None),
            P("dp", "ctx", None),
            P(),
            P(),
        ),
        out_specs=(P("dp", "ctx", None), P("dp", "ctx", None), P("dp", "ctx", None), P()),
        check_vma=False,
    )
```

time: 133 us -> 118 us (0.89)
  Pallas kernels: 126 us -> 117 us
  local copies, waits for them, and re-layouts: 6.55 us -> 0 us
    pallas_call x1, Pallas kernels: 126 us -> 114 us  [gradients(): pl.pallas_call(kernel, out_shape=[jax.ShapeDtypeStruct((1, ROWS, SSM_HEAD...]
    unnamed x10 -> x0, local copies, waits for them, and re-layouts: 5.76 us -> none
    pallas_call x0 -> x1, Pallas kernels: none -> 2.4 us  [settle(): pl.pallas_call(settle_kernel, out_shape=[narrow, narrow, jax.ShapeDtypeSt...]
where the time goes in v3:
time: 118 us; the launch traced here: 117 us
  Pallas kernels  117 us (99%)
    pallas_call x1, Pallas kernels, gradients(): pl.pallas_call(kernel, out_shape=[jax.ShapeDtypeStruct((1, ROWS, SSM_HEAD...  114 us
    pallas_call x1, Pallas kernels, settle(): pl.pallas_call(settle_kernel, out_shape=[narrow, narrow, jax.ShapeDtypeSt...  2.4 us

profile of v3, /device:TPU:1, one launch (start us, length us, event | category | flops | bytes accessed | tf_op | source)
XLA Modules:
  0.0 117.3 jit_solution(17257393581731429672)
XLA Ops:
  0.6 114.3 %gradients.1 = (bf16[1,128,4096]{2,1,0:T(8,128)(2,1)}, bf16[2,128,512]{2,1,0:T(8,128)(2,1)}, f32[2,128]{1,0:T(2,128)}) custom-call(bf16[1,128,4096]{2,1,0:T(8,128)(2,1)} %q.1, bf16[1,128,4096]{2,1,0:T(8,128)(2,1)} %dvm.1, bf16[1,128,512]{2,1,0:T(8,128)(2,1)} %k.1, bf16[1,128,512]{2,1,0:T(8,128)(2,1)} %v.1, bf16[1,128,4096]{2,1,0:T(8,128)(2,1)} %x.1, ...), custom_call_target="tpu_custom_call" | custom-call | tf_op jit(solution)/shard_map/gradients/pallas_call | solution.py:773
  114.9 2.4 %settle.1 = (bf16[1,128,512]{2,1,0:T(8,128)(2,1)}, bf16[1,128,512]{2,1,0:T(8,128)(2,1)}, bf16[1,128,4096]{2,1,0:T(8,128)(2,1)}, f32[2,128]{1,0:T(2,128)}) custom-call(bf16[1,128,4096]{2,1,0:T(8,128)(2,1)} %get-tuple-element.7.x, bf16[2,128,512]{2,1,0:T(8,128)(2,1)} %get-tuple-element.8.kv, f32[2,128]{1,0:T(2,128)} %get-tuple-element.9.dec), custom_call_target="tpu_custom_call" | custom-call | tf_op jit(solution)/shard_map/settle/pallas_call | solution.py:800

commit v4 on v3

--- a/solution.py
+++ b/solution.py
@@ -87,47 +87,35 @@
 
 
 def pack_small(out_grad, saved, ids, step, alog, small):
-    ones = jnp.ones((8, HEAD_DIM), F32)
-    sub = lax.broadcasted_iota(jnp.int32, (8, ROWS), 0)
-    docs = jnp.broadcast_to(ids[...].astype(F32), (8, ROWS))
+    docs = jnp.broadcast_to(ids[...].astype(F32), (4, ROWS))
     rate = step[0] * -jnp.exp(alog[...])
     upto = lax.broadcasted_iota(jnp.int32, (ROWS, ROWS), 0) <= lax.broadcasted_iota(jnp.int32, (ROWS, ROWS), 1)
     totals = dot(rate, upto.astype(F32), TN, HIGHEST)
     steps = step[0].T
+    lane = lax.broadcasted_iota(jnp.int32, (ROWS, ROWS), 1)
+    deltas = jnp.zeros((ROWS, ROWS), F32)
+    for h in range(QHEADS):
+        cols = slice(h * HEAD_DIM, (h + 1) * HEAD_DIM)
+        product = out_grad[0, :, cols].astype(F32) * saved[0, :, cols].astype(F32)
+        deltas = jnp.where(lane == h, jnp.sum(product, axis=1, keepdims=True), deltas)
+    deltas = deltas.T
     for j in range(CTX):
         at = 8 * slot(j)
         small[j, 0:8, :] = steps[at : at + 8]
         small[j, 8:16, :] = totals[at : at + 8]
-
-    def one(pair, _):
-        tile = docs
-        for e in range(4):
-            cols = columns(4 * pair + e, HEAD_DIM)
-            product = out_grad[0, :, cols].astype(F32) * saved[0, :, cols].astype(F32)
-            tile = jnp.where(sub == e, dot(ones, product, NT, HIGHEST), tile)
-        for z in range(2):
-            small[pair // 2 * 4 + 2 * z + pair % 2, 16:24, :] = tile
-        return 0
-
-    lax.fori_loop(0, CTX // 2, one, 0)
-
-
-def spread_columns(small, zz, dcol, doccol):
-    row = lax.broadcasted_iota(jnp.int32, (24, 5 * ROWS), 0) % 8
-    lane = lax.broadcasted_iota(jnp.int32, (24, 5 * ROWS), 1) // ROWS
-    pick = jnp.where(row == lane, 1.0, 0.0).astype(BF16)
+        pair = 4 * (j // 4 * 2 + j % 2)
+        small[j, 16:20, :] = deltas[pair : pair + 4]
+        small[j, 20:24, :] = docs
+
+
+def spread_columns(small, doccol):
     doccol[0:8, :] = jnp.full((8, ROWS), -1.0, F32)
+    row = lax.broadcasted_iota(jnp.int32, (8, ROWS), 0)
+    pick = jnp.where(row == 4, 1.0, 0.0).astype(BF16)
 
     def one(src, _):
-        parts = jnp.concatenate([p.astype(F32) for p in three(small[src, 16:24, :])], axis=0).astype(BF16)
-        wide = dot(parts, pick, TN)
-        doccol[pl.ds(pl.multiple_of(8 + src * ROWS, 8), ROWS), :] = wide[:, 4 * ROWS :]
-
-        @pl.when(src // 2 % 2 == zz)
-        def _():
-            dcol[query_rows(src, 0), :] = wide[:HALF, : 4 * ROWS]
-            dcol[query_rows(src, 1), :] = wide[HALF:, : 4 * ROWS]
-
+        docs = jnp.where(row == 4, small[src, 16:24, :], 0.0).astype(BF16)
+        doccol[pl.ds(pl.multiple_of(8 + src * ROWS, 8), ROWS), :] = dot(docs, pick, TN)
         return 0
 
     lax.fori_loop(0, CTX, one, 0)
@@ -139,65 +127,91 @@
     return pl.ds(pl.multiple_of(block * ROWS + second * HALF, HALF), HALF)
 
 
-def attention_block(i, off, q, d, kv, small, dcol, doccol, dkv, q2, d2, s_ref, m_ref, l_ref, dq):
+def transpose_keys(kv, kt):
+    def one(n, _):
+        rows = device_rows(n)
+        kt[:, rows] = kv[0, rows, :].T
+        return 0
+
+    lax.fori_loop(0, CTX, one, 0)
+
+
+def attention_block(i, off, zz, q, d, kv, kt, small, doccol, dkv, q2, d2, qt, dt, s_ref, dq, whole):
     rows = device_rows(i)
     for h in range(4):
         part = pl.ds(h * ROWS, ROWS)
         q2[part, :] = q[rows, h * HEAD_DIM : (h + 1) * HEAD_DIM]
         d2[part, :] = d[rows, h * HEAD_DIM : (h + 1) * HEAD_DIM]
-    m_ref[...] = jnp.full(m_ref.shape, FAR, F32)
-    l_ref[...] = jnp.zeros(l_ref.shape, F32)
+        qt[:, part] = q[rows, h * HEAD_DIM : (h + 1) * HEAD_DIM].T
+        dt[:, part] = d[rows, h * HEAD_DIM : (h + 1) * HEAD_DIM].T
     dq[...] = jnp.zeros(dq.shape, F32)
     first = jnp.maximum(i - (SPAN - 1), 0)
-    ahead = lax.broadcasted_iota(jnp.int32, (ROWS, BLOCK), 0) - lax.broadcasted_iota(jnp.int32, (ROWS, BLOCK), 1)
-
-    def scores(j, _):
+
+    def each(body, carry):
+        if not whole:
+            return lax.fori_loop(0, i + 1 - first, body, carry)
+        for n in range(SPAN):
+            carry = body(n, carry)
+        return carry
+
+    ahead = lax.broadcasted_iota(jnp.int32, (BLOCK, ROWS), 1) - lax.broadcasted_iota(jnp.int32, (BLOCK, ROWS), 0)
+    own = small[2 * i + off // ROWS, 20:21, :]
+    late = i // 4
+    plane = i + late * (7 - 2 * i)
+    base = 4 * plane + 2 * zz
+    lo, hi = small[base + late, 16:24, :], small[base + 1 - late, 16:24, :]
+    left = lax.broadcasted_iota(jnp.int32, (8, ROWS), 1) < HALF
+    early_tile = jnp.where(left, lo, jnp.roll(hi, HALF, 1))
+    late_tile = jnp.where(left, jnp.roll(lo, HALF, 1), hi)
+    tile = jnp.where(late == 1, late_tile, early_tile)
+    delta = jnp.concatenate([tile[h : h + 1, :] for h in range(4)], axis=1)
+
+    def scores(n, m):
+        j = first + n
         keys = kv[0, block_rows(j), :]
-        own = doccol[pl.ds(pl.multiple_of(8 + i * BLOCK + off, 8), ROWS), :]
-        own = jnp.concatenate([own, own], axis=1)
-        theirs = jnp.concatenate([small[2 * j, 20:21, :], small[2 * j + 1, 20:21, :]], axis=1)
+        theirs = doccol[pl.ds(pl.multiple_of(8 + j * BLOCK, 8), BLOCK), :]
         allowed = (own == theirs) & (ahead >= (j - i) * BLOCK - off)
-        for h in range(4):
-            part = pl.ds(h * ROWS, ROWS)
-            s = jnp.where(allowed, dot(q2[part, :], keys, NT), FAR)
-            s_ref[j - first, part, :] = s
-            m_ref[part, :] = jnp.maximum(m_ref[part, :], jnp.maximum(s[:, :ROWS], s[:, ROWS:]))
-        return 0
-
-    lax.fori_loop(first, i + 1, scores, 0)
-    m_ref[...] = jnp.broadcast_to(jnp.max(m_ref[...], axis=1, keepdims=True), m_ref.shape)
-
-    def exps(j, _):
-        for h in range(4):
-            part = pl.ds(h * ROWS, ROWS)
-            m = m_ref[part, :]
-            e = jnp.exp((s_ref[j - first, part, :] - jnp.concatenate([m, m], axis=1)) * SCALE)
-            s_ref[j - first, part, :] = e
-            l_ref[part, :] += e[:, :ROWS] + e[:, ROWS:]
-        return 0
-
-    lax.fori_loop(first, i + 1, exps, 0)
-    l_ref[...] = jnp.broadcast_to(1.0 / jnp.sum(l_ref[...], axis=1, keepdims=True), l_ref.shape)
-
-    def grads(j, _):
+        parts = []
+        for half in range(2):
+            s = dot(keys, qt[:, pl.ds(half * BLOCK, BLOCK)], NN)
+            s = jnp.where(jnp.concatenate([allowed, allowed], axis=1), s, FAR)
+            s_ref[n, :, pl.ds(half * BLOCK, BLOCK)] = s
+            parts.append(jnp.max(s.reshape(BLOCK // 8, 8, BLOCK), axis=0))
+        return jnp.maximum(m, jnp.concatenate(parts, axis=1))
+
+    m = each(scores, jnp.full((8, 4 * ROWS), FAR, F32))
+    m = jnp.max(m, axis=0, keepdims=True)
+
+    def exps(n, total):
+        parts = []
+        for half in range(2):
+            cols = pl.ds(half * BLOCK, BLOCK)
+            e = jnp.exp((s_ref[n, :, cols] - m[:, half * BLOCK : (half + 1) * BLOCK]) * SCALE)
+            s_ref[n, :, cols] = e
+            parts.append(jnp.sum(e.reshape(BLOCK // 8, 8, BLOCK), axis=0))
+        return total + jnp.concatenate(parts, axis=1)
+
+    total = each(exps, jnp.zeros((8, 4 * ROWS), F32))
+    inv = 1.0 / jnp.sum(total, axis=0, keepdims=True)
+
+    def grads(n, _):
+        j = first + n
         there = block_rows(j)
-        keys, vals = kv[0, there, :], kv[1, there, :]
+        vals, keys_t = kv[1, there, :], kt[:, there]
         probs, scaled = [], []
-        for h in range(4):
-            part = pl.ds(h * ROWS, ROWS)
-            inv = l_ref[part, :]
-            p = s_ref[j - first, part, :] * jnp.concatenate([inv, inv], axis=1)
-            delta = dcol[rows, h * ROWS : (h + 1) * ROWS]
-            dp = dot(d2[part, :], vals, NT) - jnp.concatenate([delta, delta], axis=1)
+        for half in range(4):
+            cols = slice(half * ROWS, (half + 1) * ROWS)
+            p = s_ref[n, :, pl.ds(half * ROWS, ROWS)] * inv[:, cols]
+            dp = dot(vals, dt[:, pl.ds(half * ROWS, ROWS)], NN) - delta[:, cols]
             ds = (p * dp * SCALE).astype(BF16)
-            dq[part, :] += dot(ds, keys, NN)
+            dq[:, cols] += dot(keys_t, ds, NN)
             probs.append(p.astype(BF16))
             scaled.append(ds)
-        dkv[0, there, :] += dot(jnp.concatenate(scaled, axis=0), q2[...], TN)
-        dkv[1, there, :] += dot(jnp.concatenate(probs, axis=0), d2[...], TN)
+        dkv[0, there, :] += dot(jnp.concatenate(scaled, axis=1), q2[...], NN)
+        dkv[1, there, :] += dot(jnp.concatenate(probs, axis=1), d2[...], NN)
         return 0
 
-    lax.fori_loop(first, i + 1, grads, 0)
+    each(grads, 0)
 
 
 def spread_matrix(spread):
@@ -297,7 +311,7 @@
            lq, ld, lkv, lbc, lx, ls, small,
            x_in_send, x_in_recv, small_send, small_recv, first_send, first_recv,
            z_send, core_send, relay_send, fwd_recv, q_send, q_recv, own_sem,
-           dkv, q2, d2, s_ref, m_ref, l_ref, dq, dcol, doccol, spread, gstate, gtimed, acc_a, acc_s, skip,
+           dkv, q2, d2, qt, dt, kt, s_ref, dq, doccol, spread, gstate, gtimed, acc_a, acc_s, skip,
            dx, x_send, x_recv, x_own,
            cot, cot_out, cot_send, cot_recv,
            pair_in, pair_send, pair_recv, half_out, half_in, half_send, half_recv,
@@ -410,11 +424,16 @@
     own = own_copies()
     for copy in own[:-1]:
         copy.start()
+    send_first((4, 5))
     send_q(1)
-    send_first((4, 5))
     pack_small(dvm, o, ids, step, alog, small)
     to_all(lambda to: small_copy(to, me, to).start())
     own[-1].start()
+
+    @pl.when(me >= CTX // 2)
+    def _():
+        to_all(lambda to: x_in_copy(to, me, to).start())
+
     for copy in own:
         copy.wait()
 
@@ -441,19 +460,13 @@
         each_x(one)
 
     pass_on((0, 1, 2, 3), (KV_EARLY, KV_LATE))
-
-    @pl.when(me >= CTX // 2)
-    def _():
-        to_all(lambda to: x_in_copy(to, me, to).start())
-
+    pass_on((4, 5), (BC,))
+    relay((KV_EARLY, KV_LATE))
     send_q(0)
 
     @pl.when(me < CTX // 2)
     def _():
         to_all(lambda to: x_in_copy(to, me, to).start())
-
-    pass_on((4, 5), (BC,))
-    relay((KV_EARLY, KV_LATE))
 
     for ref in (dkv, gstate, gtimed, acc_a, acc_s):
         ref[...] = jnp.zeros(ref.shape, F32)
@@ -461,7 +474,7 @@
     spread_matrix(spread)
 
     to_all(lambda src: small_copy(me, src, src).wait_recv())
-    spread_columns(ls, zz, dcol, doccol)
+    spread_columns(ls, doccol)
 
     def from_core(parts):
         def one(src):
@@ -474,6 +487,7 @@
 
     from_core((KV_EARLY, KV_LATE))
     relay((BC,))
+    transpose_keys(lkv, kt)
 
     def x_copy(to, frm, peer):
         return remote(dx.at[device_rows(to), :], grad_x.at[0, :, columns(slot(frm), WIDTH)],
@@ -554,18 +568,20 @@
                 for r in range(2):
                     q_arrived(4 * i + 2 * zz + r, 0)
 
-            attention_block(i, off, lq, ld, lkv, ls, dcol, doccol, dkv, q2, d2, s_ref, m_ref, l_ref, dq)
+            for whole in (True, False):
+                @pl.when((i >= SPAN - 1) == whole)
+                def _():
+                    attention_block(i, off, zz, lq, ld, lkv, kt, ls, doccol, dkv, q2, d2, qt, dt, s_ref, dq, whole)
+
             pair_copy(i, 1 - cc).start()
             here = pl.ds(pl.multiple_of(i * BLOCK + off, ROWS), ROWS)
             for e in range(2):
                 cols = slice(e * HEAD_DIM, (e + 1) * HEAD_DIM)
-                mine = pl.ds(pl.multiple_of((2 * zz + e) * ROWS, ROWS), ROWS)
-                theirs = pl.ds(pl.multiple_of((2 - 2 * zz + e) * ROWS, ROWS), ROWS)
-                cot[here, cols] = dq[mine, :].astype(BF16)
-                cot_out[i, :, cols] = dq[theirs, :].astype(BF16)
+                cot[here, cols] = dq[:, columns(2 * zz + e, ROWS)].T.astype(BF16)
+                cot_out[i, :, cols] = dq[:, columns(2 - 2 * zz + e, ROWS)].T.astype(BF16)
             cot_copy(i, off).start()
 
-        @pl.when(n == 0)
+        @pl.when(n == 1)
         def _():
             from_core((BC,))
 
@@ -723,11 +739,11 @@
     pltpu.VMEM((2, SEQ, HEAD_DIM), F32),
     pltpu.VMEM((4 * ROWS, HEAD_DIM), BF16),
     pltpu.VMEM((4 * ROWS, HEAD_DIM), BF16),
-    pltpu.VMEM((SPAN, 4 * ROWS, BLOCK), F32),
-    pltpu.VMEM((4 * ROWS, ROWS), F32),
-    pltpu.VMEM((4 * ROWS, ROWS), F32),
-    pltpu.VMEM((4 * ROWS, HEAD_DIM), F32),
-    pltpu.VMEM((SEQ // 2, 4 * ROWS), F32),
+    pltpu.VMEM((HEAD_DIM, 4 * ROWS), BF16),
+    pltpu.VMEM((HEAD_DIM, 4 * ROWS), BF16),
+    pltpu.VMEM((HEAD_DIM, SEQ), BF16),
+    pltpu.VMEM((SPAN, BLOCK, 4 * ROWS), F32),
+    pltpu.VMEM((HEAD_DIM, 4 * ROWS), F32),
     pltpu.VMEM((SEQ + 8, ROWS), F32),
     pltpu.VMEM((48, 1536), BF16),
     pltpu.VMEM((STATE, WIDTH), F32),

time: 118 us -> 108 us (0.915)
  Pallas kernels: 117 us -> 107 us
    pallas_call x1, Pallas kernels: 114 us -> 105 us  [gradients(): pl.pallas_call(kernel, out_shape=[jax.ShapeDtypeStruct((1, ROWS, SSM_HEAD...]
where the time goes in v4:
time: 108 us
  Pallas kernels  107 us (99%)
    pallas_call x1, Pallas kernels, gradients(): pl.pallas_call(kernel, out_shape=[jax.ShapeDtypeStruct((1, ROWS, SSM_HEAD...  105 us
    pallas_call x1, Pallas kernels, settle(): pl.pallas_call(settle_kernel, out_shape=[narrow, narrow, jax.ShapeDtypeSt...  2.4 us

profile of v4, /device:TPU:1, one launch (start us, length us, event | category | flops | bytes accessed | tf_op | source)
XLA Modules:
  0.0 108.1 jit_solution(13911741296949053420)
XLA Ops:
  0.6 105.1 %gradients.1 = (bf16[1,128,4096]{2,1,0:T(8,128)(2,1)}, bf16[2,128,512]{2,1,0:T(8,128)(2,1)}, f32[2,128]{1,0:T(2,128)}) custom-call(bf16[1,128,4096]{2,1,0:T(8,128)(2,1)} %q.1, bf16[1,128,4096]{2,1,0:T(8,128)(2,1)} %dvm.1, bf16[1,128,512]{2,1,0:T(8,128)(2,1)} %k.1, bf16[1,128,512]{2,1,0:T(8,128)(2,1)} %v.1, bf16[1,128,4096]{2,1,0:T(8,128)(2,1)} %x.1, ...), custom_call_target="tpu_custom_call" | custom-call | tf_op jit(solution)/shard_map/gradients/pallas_call | solution.py:789
  105.7 2.4 %settle.1 = (bf16[1,128,512]{2,1,0:T(8,128)(2,1)}, bf16[1,128,512]{2,1,0:T(8,128)(2,1)}, bf16[1,128,4096]{2,1,0:T(8,128)(2,1)}, f32[2,128]{1,0:T(2,128)}) custom-call(bf16[1,128,4096]{2,1,0:T(8,128)(2,1)} %get-tuple-element.7.x, bf16[2,128,512]{2,1,0:T(8,128)(2,1)} %get-tuple-element.8.kv, f32[2,128]{1,0:T(2,128)} %get-tuple-element.9.dec), custom_call_target="tpu_custom_call" | custom-call | tf_op jit(solution)/shard_map/settle/pallas_call | solution.py:816

commit v5 on v4

--- a/solution.py
+++ b/solution.py
@@ -224,11 +224,10 @@
     spread[...] = jnp.where(a | b | c, 1.0, 0.0).astype(BF16)
 
 
-def ssm_chunk(c, x, bcm, small, doccol, cot, skip, spread, gstate, gtimed, acc_a, acc_s, dx):
+def ssm_chunk(c, bcm, small, doccol, cot, skip, spread, gstate, gtimed, timed_out, dx):
     base = pl.multiple_of(c * ROWS, ROWS)
     here = pl.ds(base, ROWS)
     bc, cc = bcm[0, here, :], bcm[1, here, :]
-    xc = x[here, :].astype(F32)
     dyb = cot[here, :]
     dy = dyb.astype(F32)
     steps, totals = small[c, 0:8, :], small[c, 8:16, :]
@@ -276,8 +275,7 @@
     got = intra + leave * inter[:, :WIDTH]
     got_t = intra_t + leave * (left_time * inter[:, :WIDTH] + inter[:, WIDTH:])
     dx[here, :] = (se * got + skip[0:1, :] * dy).astype(BF16)
-    acc_a[...] += se * xc * got_t
-    acc_s[...] += dy * xc
+    timed_out[here, :] = se * got_t
 
     enter = jnp.where(docs2 == before2, jnp.exp(te), 0.0)
     dye = dy * enter
@@ -303,16 +301,17 @@
 
 
 BLOCKS = SEQ // BLOCK
+LAG = 1
 KV_EARLY, KV_LATE, BC = range(3)
 
 
 def kernel(q, d, k, v, x, b, c, dvm, o, ids, step, alog, skip_in,
-           grad_x, grad_kv, grad_d,
-           lq, ld, lkv, lbc, lx, ls, small,
-           x_in_send, x_in_recv, small_send, small_recv, first_send, first_recv,
+           grad_x, grad_kv, grad_d, lx, hop, pass_x,
+           lq, ld, lkv, lbc, xv, xv_sem, ls, small,
+           x_in_send, x_in_recv, hop_send, hop_recv, hop_on_send, small_send, small_recv, first_send, first_recv,
            z_send, core_send, relay_send, fwd_recv, q_send, q_recv, own_sem,
-           dkv, q2, d2, qt, dt, kt, s_ref, dq, doccol, spread, gstate, gtimed, acc_a, acc_s, skip,
-           dx, x_send, x_recv, x_own,
+           dkv, q2, d2, qt, dt, kt, s_ref, dq, doccol, spread, gstate, gtimed, timed, acc_a, acc_s, skip,
+           dx, x_send, x_recv, x_own, pass_send, pass_recv, pass_on_send,
            cot, cot_out, cot_send, cot_recv,
            pair_in, pair_send, pair_recv, half_out, half_in, half_send, half_recv,
            done, done_send, done_recv, done_own,
@@ -413,7 +412,7 @@
             for late in range(2):
                 moves.append((((q, d)[array]).at[0, pl.ds(late * HALF, HALF), columns(xx * 2 + cc, QCOLS)],
                               ((lq, ld)[array]).at[query_rows(me, late), :]))
-        moves.append((x.at[0, :, columns(slot(me), WIDTH)], lx.at[device_rows(me), :]))
+        moves.append((x.at[0, :, columns(slot(me), WIDTH)], xv.at[device_rows(me), :]))
         moves.append((small.at[me], ls.at[me]))
         return [pltpu.make_async_copy(src, dst, own_sem.at[n]) for n, (src, dst) in enumerate(moves)]
 
@@ -424,20 +423,48 @@
     own = own_copies()
     for copy in own[:-1]:
         copy.start()
-    send_first((4, 5))
-    send_q(1)
+
+    def direct_x_in(over, flip_z, flip_c):
+        to = lax.rem(xx + over, 4) * 4 + 2 * lax.rem(zz + flip_z, 2) + lax.rem(cc + flip_c, 2)
+        return x_in_copy(to, me, to)
+
+    def hop_copy(over, core):
+        to = lax.rem(xx + over, 4) * 4 + 2 - 2 * zz + core
+        return remote(x.at[0, :, columns(slot(to), WIDTH)], hop.at[over - 1, core],
+                      hop_send.at[over - 1, core], hop_recv.at[over - 1, core], z_peer)
+
+    def hop_on(over, core):
+        to = lax.rem(xx + over, 4) * 4 + 2 * zz + core
+        return remote(hop.at[over - 1, core], lx.at[device_rows(z_peer), :],
+                      hop_on_send.at[over - 1, core], x_in_recv.at[z_peer], to)
+
+    direct_x_in(0, 1, 0).start()
+    direct_x_in(0, 1, 1).start()
+
+    @pl.when(xx >= 2)
+    def _():
+        send_first((4, 5))
+
     pack_small(dvm, o, ids, step, alog, small)
     to_all(lambda to: small_copy(to, me, to).start())
     own[-1].start()
-
-    @pl.when(me >= CTX // 2)
+    send_q(1)
+
+    @pl.when(xx < 2)
     def _():
-        to_all(lambda to: x_in_copy(to, me, to).start())
+        send_first((4, 5))
 
     for copy in own:
         copy.wait()
 
-    def pass_on(kinds, parts):
+    def planes(first, count, body):
+        def one(n, _):
+            body(n * 4 + zc)
+            return 0
+
+        lax.fori_loop(first, first + count, one, 0)
+
+    def pass_on(kinds, parts, first, count):
         def one(src):
             @pl.when(src != me)
             def _():
@@ -448,46 +475,43 @@
                 forward(part, src, z_send, z_peer).start()
                 forward(part, src, core_send, core_peer).start()
 
-        each_x(one)
-
-    def relay(parts):
+        planes(first, count, one)
+
+    def relay(parts, first, count):
         def one(src):
             src = src + 2 - 4 * zz
             for part in parts:
                 forward(part, src, z_send, z_peer).wait_recv()
                 forward(part, src, relay_send, core_peer).start()
 
-        each_x(one)
-
-    pass_on((0, 1, 2, 3), (KV_EARLY, KV_LATE))
-    pass_on((4, 5), (BC,))
-    relay((KV_EARLY, KV_LATE))
-    send_q(0)
-
-    @pl.when(me < CTX // 2)
-    def _():
-        to_all(lambda to: x_in_copy(to, me, to).start())
-
-    for ref in (dkv, gstate, gtimed, acc_a, acc_s):
-        ref[...] = jnp.zeros(ref.shape, F32)
-    skip[...] = dot(jnp.broadcast_to(skip_in[...], (8, SSM_HEADS)), own_heads(me), NN, HIGHEST)
-    spread_matrix(spread)
-
-    to_all(lambda src: small_copy(me, src, src).wait_recv())
-    spread_columns(ls, doccol)
-
-    def from_core(parts):
+        planes(first, count, one)
+
+    def from_core(parts, first, count):
         def one(src):
             for flip in (0, 1):
                 at = src + 1 - 2 * cc + flip * (2 - 4 * zz)
                 for part in parts:
                     forward(part, at, core_send, core_peer).wait_recv()
 
-        each_x(one)
-
-    from_core((KV_EARLY, KV_LATE))
-    relay((BC,))
+        planes(first, count, one)
+
+    pass_on((0, 1, 2, 3), (KV_EARLY, KV_LATE), 0, 4)
+    pass_on((4, 5), (BC,), 2, 2)
+    send_q(0)
+    for over in range(1, 4):
+        for core in range(2):
+            hop_copy(over, core).start()
+
+    for ref in (dkv, gstate, gtimed, acc_a, acc_s):
+        ref[...] = jnp.zeros(ref.shape, F32)
+    skip[...] = dot(jnp.broadcast_to(skip_in[...], (8, SSM_HEADS)), own_heads(me), NN, HIGHEST)
+    spread_matrix(spread)
+    relay((KV_EARLY, KV_LATE), 0, 4)
+    to_all(lambda src: small_copy(me, src, src).wait_recv())
+    spread_columns(ls, doccol)
+    from_core((KV_EARLY, KV_LATE), 0, 4)
     transpose_keys(lkv, kt)
+    relay((BC,), 2, 2)
 
     def x_copy(to, frm, peer):
         return remote(dx.at[device_rows(to), :], grad_x.at[0, :, columns(slot(frm), WIDTH)],
@@ -495,6 +519,20 @@
 
     def x_mine():
         return pltpu.make_async_copy(dx.at[device_rows(me), :], grad_x.at[0, :, columns(slot(me), WIDTH)], x_own)
+
+    def pass_copy(i):
+        return remote(dx.at[block_rows(i), :], pass_x.at[i // 2], pass_send.at[i // 2], pass_recv.at[i // 2], z_peer)
+
+    def passed_copy(i, sub):
+        owner = 2 * i + sub
+        return remote(pass_x.at[i // 2, pl.ds(sub * ROWS, ROWS), :], grad_x.at[0, :, columns(slot(z_peer), WIDTH)],
+                      pass_on_send.at[i // 2, sub], x_recv.at[z_peer], owner)
+
+    def passes(i):
+        return (i % 2 != zz) & (i // 2 != xx) & (i >= 2)
+
+    def passed(i):
+        return (i % 2 == zz) & (i // 2 != xx) & (i >= 2)
 
     def own_off(i):
         late = i // 4
@@ -581,11 +619,42 @@
                 cot_out[i, :, cols] = dq[:, columns(2 - 2 * zz + e, ROWS)].T.astype(BF16)
             cot_copy(i, off).start()
 
+        @pl.when(n == 0)
+        def _():
+            pass_on((4, 5), (BC,), 0, 2)
+            direct_x_in(0, 0, 1).start()
+
+        @pl.when((n >= 1) & (n < 4))
+        def _():
+            direct_x_in(n, 0, 0).start()
+            direct_x_in(n, 0, 1).start()
+
+        @pl.when((n >= 4) & (n < 7))
+        def _():
+            for core in range(2):
+                hop_copy(n - 3, core).wait_recv()
+                hop_on(n - 3, core).start()
+
+        @pl.when((n >= 2) & passed(BLOCKS + 1 - n))
+        def _():
+            i = BLOCKS + 1 - n
+            pass_copy(i).wait_recv()
+            for sub in range(2):
+                passed_copy(i, sub).start()
+
         @pl.when(n == 1)
         def _():
-            from_core((BC,))
-
-        @pl.when(n >= 1)
+            from_core((BC,), 2, 2)
+
+        @pl.when(n == 2)
+        def _():
+            relay((BC,), 0, 2)
+
+        @pl.when(n == 4)
+        def _():
+            from_core((BC,), 0, 2)
+
+        @pl.when((n >= 1) & (n <= BLOCKS))
         def _():
             sum_pair(BLOCKS - n)
 
@@ -593,20 +662,16 @@
         def _():
             sum_half(BLOCKS + 1 - n)
 
-        @pl.when(n >= 1)
-        def _():
-            i = BLOCKS - n
+        @pl.when(n >= LAG)
+        def _():
+            i = BLOCKS - 1 + LAG - n
             cot_copy(i, ROWS - own_off(i)).wait_recv()
             for sub in (1, 0):
                 owner = 2 * i + sub
 
-                @pl.when(owner != me)
-                def _():
-                    x_in_copy(me, owner, owner).wait_recv()
-
-                ssm_chunk(owner, lx, lbc, ls, doccol, cot, skip, spread, gstate, gtimed, acc_a, acc_s, dx)
-
-                @pl.when(owner != me)
+                ssm_chunk(owner, lbc, ls, doccol, cot, skip, spread, gstate, gtimed, timed, dx)
+
+                @pl.when((owner != me) & jnp.logical_not(passes(i)))
                 def _():
                     x_copy(owner, me, owner).start()
 
@@ -614,10 +679,32 @@
                 def _():
                     x_mine().start()
 
+            @pl.when(passes(i))
+            def _():
+                pass_copy(i).start()
+
         return 0
 
-    lax.fori_loop(0, BLOCKS + 1, block, 0)
-
+    lax.fori_loop(0, BLOCKS + LAG, block, 0)
+
+    def take_in(src):
+        return pltpu.make_async_copy(lx.at[device_rows(src), :], xv.at[device_rows(src), :], xv_sem.at[src])
+
+    def landed_x(src):
+        x_in_copy(me, src, src).wait_recv()
+        take_in(src).start()
+
+    to_all(landed_x)
+    to_all(lambda src: take_in(src).wait())
+
+    def gather(c, _):
+        here = device_rows(c)
+        xc = xv[here, :].astype(F32)
+        acc_a[...] += xc * timed[here, :]
+        acc_s[...] += xc * cot[here, :].astype(F32)
+        return 0
+
+    lax.fori_loop(0, CTX, gather, 0)
     decay[...] = finish_decay(me, acc_a, acc_s)
 
     def ctx_copy(frm, peer):
@@ -647,11 +734,23 @@
 
     def sent(to):
         small_copy(to, me, to).wait_send()
-        x_in_copy(to, me, to).wait_send()
-        x_copy(to, me, to).wait_send()
+
+        @pl.when(jnp.logical_not(passes(to // 2)))
+        def _():
+            x_copy(to, me, to).wait_send()
+
         ctx_copy(me, to).wait_send()
 
     to_all(sent)
+    for over in range(4):
+        for core in range(2):
+            if over:
+                hop_copy(over, core).wait_send()
+                hop_on(over, core).wait_send()
+            else:
+                direct_x_in(0, 1, core).wait_send()
+            if over or core:
+                direct_x_in(over, 0, core).wait_send()
     others_x(lambda to: [first_copy(kind, to, me, to).wait_send() for kind in range(6)])
 
     def forwarded(src):
@@ -673,6 +772,15 @@
     lax.fori_loop(1, 8, sent_q, 0)
 
     def sent_blocks(i, _):
+        @pl.when(passes(i))
+        def _():
+            pass_copy(i).wait_send()
+
+        @pl.when(passed(i))
+        def _():
+            for sub in range(2):
+                passed_copy(i, sub).wait_send()
+
         cot_copy(i, own_off(i)).wait_send()
         pair_copy(i, 1 - cc).wait_send()
         half_copy(i).wait_send()
@@ -721,10 +829,14 @@
     pltpu.VMEM((2, SEQ, HEAD_DIM), BF16),
     pltpu.VMEM((2, SEQ, STATE), BF16),
     pltpu.VMEM((SEQ, WIDTH), BF16),
+    DMA((CTX,)),
     pltpu.VMEM((CTX, 24, ROWS), F32),
     pltpu.VMEM((CTX, 24, ROWS), F32),
     DMA((CTX,)),
     DMA((CTX,)),
+    DMA((3, 2)),
+    DMA((3, 2)),
+    DMA((3, 2)),
     DMA((CTX,)),
     DMA((CTX,)),
     DMA((6, 4)),
@@ -748,6 +860,7 @@
     pltpu.VMEM((48, 1536), BF16),
     pltpu.VMEM((STATE, WIDTH), F32),
     pltpu.VMEM((STATE, WIDTH), F32),
+    pltpu.VMEM((SEQ, WIDTH), F32),
     pltpu.VMEM((ROWS, WIDTH), F32),
     pltpu.VMEM((ROWS, WIDTH), F32),
     pltpu.VMEM((8, WIDTH), F32),
@@ -755,6 +868,9 @@
     DMA((CTX,)),
     DMA((CTX,)),
     DMA,
+    DMA((4,)),
+    DMA((4,)),
+    DMA((4, 2)),
     pltpu.VMEM((SEQ, WIDTH), BF16),
     pltpu.VMEM((BLOCKS, ROWS, WIDTH), BF16),
     DMA((BLOCKS,)),
@@ -792,15 +908,18 @@
             jax.ShapeDtypeStruct((1, ROWS, SSM_HEADS * SSM_DIM), BF16),
             jax.ShapeDtypeStruct((2, ROWS, KVHEADS * HEAD_DIM), BF16),
             jax.ShapeDtypeStruct((2, SSM_HEADS), F32),
+            jax.ShapeDtypeStruct((SEQ, WIDTH), BF16),
+            jax.ShapeDtypeStruct((3, 2, ROWS, WIDTH), BF16),
+            jax.ShapeDtypeStruct((4, BLOCK, WIDTH), BF16),
         ],
         in_specs=[hbm] * 7 + [vmem] * 6,
-        out_specs=[hbm, hbm, vmem],
+        out_specs=[hbm, hbm, vmem, hbm, hbm, hbm],
         scratch_shapes=SCRATCH,
         compiler_params=pltpu.CompilerParams(
             collective_id=0, has_side_effects=True, vmem_limit_bytes=60 * 2**20
         ),
         name="gradients",
-    )(q, d, k, v, x, b, c, d, o, ids, step, alog, skip)
+    )(q, d, k, v, x, b, c, d, o, ids, step, alog, skip)[:3]
 
 
 def settle_kernel(x, kv, dec, grad_k, grad_v, grad_x, grad_d):

time: 108 us -> 102 us (0.944); the launches traced: 108 us -> 101 us
  Pallas kernels: 107 us -> 100 us
    pallas_call x1, Pallas kernels: 105 us -> 97.6 us  [gradients(): pl.pallas_call(kernel, out_shape=[jax.ShapeDtypeStruct((1, ROWS, SSM_HEAD...]
where the time goes in v5:
time: 102 us; the launch traced here: 101 us
  Pallas kernels  100 us (98%)
    pallas_call x1, Pallas kernels, gradients(): pl.pallas_call(kernel, out_shape=[jax.ShapeDtypeStruct((1, ROWS, SSM_HEAD...  97.6 us
    pallas_call x1, Pallas kernels, settle(): pl.pallas_call(settle_kernel, out_shape=[narrow, narrow, jax.ShapeDtypeSt...  2.4 us

profile of v5, /device:TPU:1, one launch (start us, length us, event | category | flops | bytes accessed | tf_op | source)
XLA Modules:
  0.0 100.7 jit_solution(14322296685216540983)
XLA Ops:
  0.6 97.6 %gradients.1 = (bf16[1,128,4096]{2,1,0:T(8,128)(2,1)}, bf16[2,128,512]{2,1,0:T(8,128)(2,1)}, f32[2,128]{1,0:T(2,128)}, bf16[2048,256]{1,0:T(8,128)(2,1)}, bf16[3...) custom-call(bf16[1,128,4096]{2,1,0:T(8,128)(2,1)} %q.1, bf16[1,128,4096]{2,1,0:T(8,128)(2,1)} %dvm.1, ...), custom_call_target="tpu_custom_call" | custom-call | tf_op jit(solution)/shard_map/gradients/pallas_call | solution.py:905
  98.3 2.4 %settle.1 = (bf16[1,128,512]{2,1,0:T(8,128)(2,1)}, bf16[1,128,512]{2,1,0:T(8,128)(2,1)}, bf16[1,128,4096]{2,1,0:T(8,128)(2,1)}, f32[2,128]{1,0:T(2,128)}) custom-call(bf16[1,128,4096]{2,1,0:T(8,128)(2,1)} %get-tuple-element.7.x, bf16[2,128,512]{2,1,0:T(8,128)(2,1)} %get-tuple-element.8.kv, f32[2,128]{1,0:T(2,128)} %get-tuple-element.9.dec), custom_call_target="tpu_custom_call" | custom-call | tf_op jit(solution)/shard_map/settle/pallas_call | solution.py:935

commit v6 on v5

--- a/solution.py
+++ b/solution.py
@@ -590,6 +590,13 @@
             def _():
                 done_mine(i, r).start()
 
+    def take_in(src):
+        return pltpu.make_async_copy(lx.at[device_rows(src), :], xv.at[device_rows(src), :], xv_sem.at[src])
+
+    def landed_x(src):
+        x_in_copy(me, src, src).wait_recv()
+        take_in(src).start()
+
     def block(n, _):
         @pl.when(n < BLOCKS)
         def _():
@@ -624,16 +631,16 @@
             pass_on((4, 5), (BC,), 0, 2)
             direct_x_in(0, 0, 1).start()
 
-        @pl.when((n >= 1) & (n < 4))
-        def _():
-            direct_x_in(n, 0, 0).start()
-            direct_x_in(n, 0, 1).start()
-
-        @pl.when((n >= 4) & (n < 7))
+        @pl.when(n < 3)
+        def _():
+            direct_x_in(n + 1, 0, 0).start()
+            direct_x_in(n + 1, 0, 1).start()
+
+        @pl.when((n >= 2) & (n < 5))
         def _():
             for core in range(2):
-                hop_copy(n - 3, core).wait_recv()
-                hop_on(n - 3, core).start()
+                hop_copy(n - 1, core).wait_recv()
+                hop_on(n - 1, core).start()
 
         @pl.when((n >= 2) & passed(BLOCKS + 1 - n))
         def _():
@@ -662,6 +669,10 @@
         def _():
             sum_half(BLOCKS + 1 - n)
 
+        @pl.when(n == BLOCKS)
+        def _():
+            to_all(landed_x)
+
         @pl.when(n >= LAG)
         def _():
             i = BLOCKS - 1 + LAG - n
@@ -687,14 +698,6 @@
 
     lax.fori_loop(0, BLOCKS + LAG, block, 0)
 
-    def take_in(src):
-        return pltpu.make_async_copy(lx.at[device_rows(src), :], xv.at[device_rows(src), :], xv_sem.at[src])
-
-    def landed_x(src):
-        x_in_copy(me, src, src).wait_recv()
-        take_in(src).start()
-
-    to_all(landed_x)
     to_all(lambda src: take_in(src).wait())
 
     def gather(c, _):

time: 102 us -> 100 us (0.980); the launches traced: 101 us -> 100 us
  no operation moved by 1% of the time
where the time goes in v6:
time: 100 us
  Pallas kernels  99.7 us (100%)
    pallas_call x1, Pallas kernels, gradients(): pl.pallas_call(kernel, out_shape=[jax.ShapeDtypeStruct((1, ROWS, SSM_HEAD...  97.3 us
    pallas_call x1, Pallas kernels, settle(): pl.pallas_call(settle_kernel, out_shape=[narrow, narrow, jax.ShapeDtypeSt...  2.4 us

profile of v6, /device:TPU:1, one launch (start us, length us, event | category | flops | bytes accessed | tf_op | source)
XLA Modules:
  0.0 100.3 jit_solution(13356134250251835051)
XLA Ops:
  0.6 97.3 %gradients.1 = (bf16[1,128,4096]{2,1,0:T(8,128)(2,1)}, bf16[2,128,512]{2,1,0:T(8,128)(2,1)}, f32[2,128]{1,0:T(2,128)}, bf16[2048,256]{1,0:T(8,128)(2,1)}, bf16[3...) custom-call(bf16[1,128,4096]{2,1,0:T(8,128)(2,1)} %q.1, bf16[1,128,4096]{2,1,0:T(8,128)(2,1)} %dvm.1, ...), custom_call_target="tpu_custom_call" | custom-call | tf_op jit(solution)/shard_map/gradients/pallas_call | solution.py:908
  97.9 2.4 %settle.1 = (bf16[1,128,512]{2,1,0:T(8,128)(2,1)}, bf16[1,128,512]{2,1,0:T(8,128)(2,1)}, bf16[1,128,4096]{2,1,0:T(8,128)(2,1)}, f32[2,128]{1,0:T(2,128)}) custom-call(bf16[1,128,4096]{2,1,0:T(8,128)(2,1)} %get-tuple-element.7.x, bf16[2,128,512]{2,1,0:T(8,128)(2,1)} %get-tuple-element.8.kv, f32[2,128]{1,0:T(2,128)} %get-tuple-element.9.dec), custom_call_target="tpu_custom_call" | custom-call | tf_op jit(solution)/shard_map/settle/pallas_call | solution.py:938

commit v7 on v6

--- a/solution.py
+++ b/solution.py
@@ -697,6 +697,7 @@
         return 0
 
     lax.fori_loop(0, BLOCKS + LAG, block, 0)
+    sum_half(0)
 
     to_all(lambda src: take_in(src).wait())
 
@@ -722,7 +723,6 @@
     to_all(lambda to: ctx_copy(me, to).start())
     ctx_mine = pltpu.make_async_copy(decay, ctx_decay.at[me], ctx_own)
     ctx_mine.start()
-    sum_half(0)
     to_all(lambda frm: ctx_copy(frm, frm).wait_recv())
     ctx_mine.wait()
     seq_decay[...] = jnp.sum(ctx_decay[...], axis=0)

time: 100 us -> 101 us (1.010)
  Pallas kernels: 99.7 us -> 101 us
where the time goes in v7:
time: 101 us
  Pallas kernels  101 us (100%)
    pallas_call x1, Pallas kernels, gradients(): pl.pallas_call(kernel, out_shape=[jax.ShapeDtypeStruct((1, ROWS, SSM_HEAD...  98.2 us
    pallas_call x1, Pallas kernels, settle(): pl.pallas_call(settle_kernel, out_shape=[narrow, narrow, jax.ShapeDtypeSt...  2.4 us

profile of v7, /device:TPU:1, one launch (start us, length us, event | category | flops | bytes accessed | tf_op | source)
XLA Modules:
  0.0 101.3 jit_solution(410137826367122467)
XLA Ops:
  0.6 98.2 %gradients.1 = (bf16[1,128,4096]{2,1,0:T(8,128)(2,1)}, bf16[2,128,512]{2,1,0:T(8,128)(2,1)}, f32[2,128]{1,0:T(2,128)}, bf16[2048,256]{1,0:T(8,128)(2,1)}, bf16[3...) custom-call(bf16[1,128,4096]{2,1,0:T(8,128)(2,1)} %q.1, bf16[1,128,4096]{2,1,0:T(8,128)(2,1)} %dvm.1, ...), custom_call_target="tpu_custom_call" | custom-call | tf_op jit(solution)/shard_map/gradients/pallas_call | solution.py:908
  98.9 2.4 %settle.1 = (bf16[1,128,512]{2,1,0:T(8,128)(2,1)}, bf16[1,128,512]{2,1,0:T(8,128)(2,1)}, bf16[1,128,4096]{2,1,0:T(8,128)(2,1)}, f32[2,128]{1,0:T(2,128)}) custom-call(bf16[1,128,4096]{2,1,0:T(8,128)(2,1)} %get-tuple-element.7.x, bf16[2,128,512]{2,1,0:T(8,128)(2,1)} %get-tuple-element.8.kv, f32[2,128]{1,0:T(2,128)} %get-tuple-element.9.dec), custom_call_target="tpu_custom_call" | custom-call | tf_op jit(solution)/shard_map/settle/pallas_call | solution.py:938
